TPU v7x, 32 devices: a whole 2x2x4 slice. The times are simulated.
32 devices in a mesh: dp: 8 (over y, x, core), mlp: 4 (over z).
Axes of the slice: x: 2, y: 2, z: 4, core: 2. Of those that a mesh axis runs over, the one named last changes fastest.
Arguments:
- tokens: float32 [16384, 1024], P(('dp', 'mlp')), may hold values from -6 to 6
- cotangent: float32 [16384, 1024], P(('dp', 'mlp')), may hold values from -6 to 6
- positions: int32 [16384], P(('dp', 'mlp')), may hold values from 0 to 511, as said below
- owners: int32 [4, 192], P('mlp'), may hold values from 0 to 191, as said below
- masters: float32 [4, 192, 128, 128], P('mlp', 'dp')
- basis_left: float32 [4, 192, 128, 128], P('mlp', 'dp'), as said below
- basis_right: float32 [4, 192, 128, 128], P('mlp', 'dp'), as said below
- moment1: float32 [4, 192, 128, 128], P('mlp', 'dp')
- moment2: float32 [4, 192, 128, 128], P('mlp', 'dp'), as said below
- ema: float32 [4, 192, 128, 128], P('mlp', 'dp')
- vectors: float32 [9, 1024], replicated, as said below
- vector_moment1: float32 [9, 1024], replicated
- vector_moment2: float32 [9, 1024], replicated, as said below
- hidden_bias: float32 [4096], replicated, may hold values from -1.8 to 1.8
- hidden_moment1: float32 [4096], replicated
- hidden_moment2: float32 [4096], replicated, as said below
Outputs:
- result: float32 [16384, 1024], P(('dp', 'mlp'))
- grad_tokens: float32 [16384, 1024], P(('dp', 'mlp'))
- block_grad: float32 [4, 192, 128, 128], P('mlp', 'dp')
- moment1_new: float32 [4, 192, 128, 128], P('mlp', 'dp')
- moment2_new: float32 [4, 192, 128, 128], P('mlp', 'dp')
- master_new: float32 [4, 192, 128, 128], P('mlp', 'dp')
- weight_copy: bfloat16 [4, 192, 128, 128], P('mlp', 'dp')
- ema_new: float32 [4, 192, 128, 128], P('mlp', 'dp')
- vector_grad: float32 [9, 1024], replicated
- vector_moment1_new: float32 [9, 1024], replicated
- vector_moment2_new: float32 [9, 1024], replicated
- vectors_new: float32 [9, 1024], replicated
- hidden_grad: float32 [4096], replicated
- hidden_moment1_new: float32 [4096], replicated
- hidden_moment2_new: float32 [4096], replicated
- hidden_new: float32 [4096], replicated
Inputs may be any that keep to these rules, and one draw needn't show every extreme that they name: Each row of owners names every slot of 0 to 191 once. Each sequence of 512 tokens is packed with documents; positions count from 0 at the first token of each document and rise by one from token to token within it; the first sequence is one document. `basis_left`: each slot is an orthogonal 128 x 128 matrix. `basis_right`: each slot is an orthogonal 128 x 128 matrix. `moment2`: positive. `vector_moment2`: positive. `hidden_moment2`: positive. `vectors`: rows 0 and 2 lie between 0.5 and 1.5.
All inputs are finite; a program needn't handle non-finite values.
Results may differ from a plain program's by a relative error of at most 0.0095.
Values may be sent and summed in bfloat16 or wider, within the bound.
A program may use at most 192 MiB of HBM per device.

v0:
```python
import functools

import jax
import jax.numpy as jnp
from jax import lax
from jax.experimental import pallas as pl
from jax.experimental.pallas import tpu as pltpu
from jax.sharding import PartitionSpec as P

HEADS = 16
HDIM = 64
ROT = 16
FF = 4096
STEP = 5
TILE = 128
LANES = 128
GROUP = 4

PRECISE = lax.Precision.HIGHEST
eps_norm = 1e-05
eps_adam = 1e-08
lr_matrix = 0.05
lr_vector = 0.5
ema_keep = 0.8

F32 = jnp.float32
BF16 = jnp.bfloat16
ANY = pl.BlockSpec(memory_space=pl.ANY)
VMEM = pl.BlockSpec(memory_space=pltpu.VMEM)
SMEM = pl.BlockSpec(memory_space=pltpu.SMEM)


def dot_nn(left, right):
    return jnp.dot(left, right, preferred_element_type=F32)


def dot_nt(left, right):
    return lax.dot_general(left, right, (((1,), (1,)), ((), ())), preferred_element_type=F32)


def dot_tn(left, right):
    return lax.dot_general(left, right, (((0,), (0,)), ((), ())), preferred_element_type=F32)


def precise(left, right, left_dim, right_dim):
    return lax.dot_general(
        left,
        right,
        (((left_dim,), (right_dim,)), ((), ())),
        precision=PRECISE,
        preferred_element_type=F32,
    )


MESH = pl.DeviceIdType.MESH


def flip(index, mask):
    bit = 1
    while bit <= mask:
        if mask & bit:
            index = index + bit - 2 * bit * ((index // bit) % 2)
        bit *= 2
    return index


def differ(left, right, count):
    total, bit = 0, 1
    while bit < count:
        one, two = (left // bit) % 2, (right // bit) % 2
        total = total + bit * (one + two - 2 * one * two)
        bit *= 2
    return total


class Links:
    def __init__(self, send_sems, recv_sems):
        self.send_sems, self.recv_sems = send_sems, recv_sems
        self.number = 0
        self.all = []

    def send(self, source, target, device):
        copy = pltpu.make_async_remote_copy(
            src_ref=source,
            dst_ref=target,
            send_sem=self.send_sems.at[self.number],
            recv_sem=self.recv_sems.at[self.number],
            device_id=device,
            device_id_type=MESH,
        )
        self.number += 1
        copy.start()
        entry = [copy, False]
        self.all.append(entry)
        return entry

    def arrived(self, entry):
        if not entry[1]:
            entry[0].wait_recv()
            entry[1] = True

    def finish(self):
        for entry in self.all:
            self.arrived(entry)
            entry[0].wait_send()


def greet(me, column, masks_dp, masks_z):
    barrier = pltpu.get_barrier_semaphore()
    for mask in masks_dp:
        pl.semaphore_signal(barrier, inc=1, device_id={"dp": flip(me, mask)}, device_id_type=MESH)
    for mask in masks_z:
        pl.semaphore_signal(
            barrier, inc=1, device_id={"mlp": flip(column, mask)}, device_id_type=MESH
        )
    pl.semaphore_wait(barrier, len(masks_dp) + len(masks_z))


def start_side(moves, send_sems, recv_sems):
    me, column = lax.axis_index("dp"), lax.axis_index("mlp")
    masks_dp = sorted({mask for _, _, axis, mask in moves if axis == "dp"})
    masks_z = sorted({mask for _, _, axis, mask in moves if axis == "mlp"})
    greet(me, column, masks_dp, masks_z)
    links = Links(send_sems, recv_sems)
    for source, target, axis, mask in moves:
        links.send(source, target, {axis: flip(me if axis == "dp" else column, mask)})
    return links


def side_shapes(moves):
    return [pltpu.SemaphoreType.DMA((moves,)), pltpu.SemaphoreType.DMA((moves,))]


class Spread:
    def __init__(self, links, slab, me, count, rows, first, size, backward):
        self.links, self.slab, self.me = links, slab, me
        self.rows, self.first, self.size = rows, first, size
        self.bits = [1 << i for i in range(1, count.bit_length() - 1)]
        if backward:
            self.bits = self.bits[::-1]
        self.came = {}
        self.order = []

    def part(self, at):
        return self.slab.at[pl.ds(at * self.rows + self.first, self.size)]

    def forward(self, at, step, source=None):
        source = self.part(at) if source is None else source
        for later in range(step, len(self.bits)):
            bit = self.bits[later]
            entry = self.links.send(source, self.part(at ^ bit), {"dp": flip(self.me, bit)})
            self.came[at ^ bit] = (entry, later + 1)
            self.order.append(at ^ bit)
        self.links.send(source, self.part(at ^ 1), {"dp": flip(self.me, 1)})

    def relay(self):
        while self.order:
            at = min(self.order, key=lambda index: (self.came[index][1], index.bit_count()))
            self.order.remove(at)
            entry, step = self.came[at]
            self.links.arrived(entry)
            self.forward(at, step)


def attn_unit(column, rank, place):
    by_columns = (place // 2) * 8 + 2 * rank + place % 2
    by_rows = (2 * rank + place // 8) * 8 + place % 8
    return jnp.where(column == 3, by_rows, by_columns)


def ff_unit(core, place):
    later = place - 32
    up = 64 + (place // 4) * 8 + core * 4 + place % 4
    down = 128 + (core * 4 + later // 8) * 8 + later % 8
    return jnp.where(place < 32, up, down)


def front_kernel(slots, devices, tokens, cot, table, masters, tile_ref, *refs):
    (hats, cots, tables, attn_parts, own_attn, own_ff, send_ff) = refs[:7]
    (slab, own_hat, own_cot, send_attn, send_sems, recv_sems, local_sems) = refs[7:]
    me, column = lax.axis_index("dp"), lax.axis_index("mlp")
    replicas = devices // 2
    core, quarter, low = me % 2, me // 2, column % 2
    links = Links(send_sems, recv_sems)
    half = slots // 2
    greet(me, column, [1] + [at << 1 for at in range(1, replicas)], [1, 2, 3])
    slab[0:slots] = masters[...].astype(BF16)
    spreads = [
        Spread(links, slab, me, devices, slots, 0, half, False),
        Spread(links, slab, me, devices, slots, half, slots - half, True),
    ]
    for spread in spreads:
        spread.forward(0, 0)

    length = tokens.shape[0]
    step_rows = 128

    def normalize(step, carry):
        where = pl.ds(pl.multiple_of(step * step_rows, step_rows), step_rows)
        value = tokens[where, :]
        value = value - jnp.mean(value, axis=-1, keepdims=True)
        value = value * lax.rsqrt(jnp.mean(value * value, axis=-1, keepdims=True) + eps_norm)
        own_hat[where, :] = value.astype(BF16)
        own_cot[where, :] = cot[where, :].astype(BF16)
        return carry

    lax.fori_loop(0, length // step_rows, normalize, 0)
    own = []
    along = []
    for number, (source, target) in enumerate(
        ((own_hat, hats), (table, tables), (own_cot, cots))
    ):
        along.append((target, links.send(source, target.at[2], {"mlp": flip(column, 1)})))
        links.send(source, target.at[1], {"dp": flip(me, 1)})
        copy = pltpu.make_async_copy(source, target.at[0], local_sems.at[number])
        copy.start()
        own.append(copy)
    for spread in spreads:
        spread.relay()
    for entry in links.all:
        if not any(entry is item for _, item in along):
            links.arrived(entry)

    def fill(out_ref, base, rows_out, first_row, unit_of):
        size = min(TILE, rows_out)

        def body(step, carry):
            row = first_row + step * size
            tile = tile_ref[unit_of(row // TILE)]
            where = pl.ds(pl.multiple_of(base + step * size, size), size)
            if size == TILE:
                out_ref[where, :] = slab[tile]
            else:
                out_ref[where, :] = slab[tile, pl.ds(pl.multiple_of(row % TILE, size), size), :]
            return carry

        lax.fori_loop(0, rows_out // size, body, 0)

    rows_attn = 16 * TILE // replicas
    across = []
    for bit in (3, 2, 1):
        rank = 2 * (flip(low, 1) if bit & 1 else low) + core
        base = (bit - 1) * rows_attn
        fill(
            send_attn,
            base,
            rows_attn,
            quarter * rows_attn,
            functools.partial(attn_unit, column, rank),
        )
        piece = pl.ds(base, rows_attn)
        across.append(
            (
                piece,
                links.send(
                    send_attn.at[piece, :],
                    attn_parts.at[0, piece, :],
                    {"mlp": flip(column, bit)},
                ),
            )
        )
    rows_ff = 64 * TILE // replicas
    fill(own_attn, 0, 16 * TILE, 0, functools.partial(attn_unit, column, 2 * low + core))
    for piece, entry in across[::-1]:
        links.arrived(entry)
        for at in range(1, replicas):
            links.send(
                attn_parts.at[0, piece, :],
                attn_parts.at[at, piece, :],
                {"dp": flip(me, at << 1)},
            )
    fill(send_ff, 0, rows_ff, quarter * rows_ff, functools.partial(ff_unit, core))
    fill(own_ff, 0, 64 * TILE, 0, functools.partial(ff_unit, core))
    for target, entry in along:
        links.arrived(entry)
        links.send(target.at[2], target.at[3], {"dp": flip(me, 1)})
    for copy in own:
        copy.wait()
    links.finish()


def front(tokens, cot, table, masters, tile_row):
    length, width = tokens.shape
    slots = masters.shape[0]
    devices = lax.axis_size("dp")
    replicas = devices // 2
    rows_attn = 16 * TILE // replicas
    count = 2 * (replicas - 1) + 2 * replicas + 9 + 3 * replicas + 3
    block = jax.ShapeDtypeStruct((4, length, width), BF16)
    flat = lambda number: jax.ShapeDtypeStruct((number, LANES), BF16)
    return pl.pallas_call(
        functools.partial(front_kernel, slots, devices),
        out_shape=[
            block,
            block,
            jax.ShapeDtypeStruct((4,) + table.shape, F32),
            jax.ShapeDtypeStruct((replicas, 3 * rows_attn, LANES), BF16),
            flat(16 * TILE),
            flat(64 * TILE),
            flat(64 * TILE // replicas),
        ],
        in_specs=[VMEM] * 4 + [SMEM],
        out_specs=[ANY] * 4 + [VMEM] * 3,
        scratch_shapes=[
            pltpu.VMEM((devices * slots, TILE, LANES), BF16),
            pltpu.VMEM((length, width), BF16),
            pltpu.VMEM((length, width), BF16),
            pltpu.VMEM((3 * rows_attn, LANES), BF16),
            pltpu.SemaphoreType.DMA((count,)),
            pltpu.SemaphoreType.DMA((count,)),
            pltpu.SemaphoreType.DMA((3,)),
        ],
        compiler_params=pltpu.CompilerParams(
            vmem_limit_bytes=32 << 20, collective_id=0, has_side_effects=True
        ),
        cost_estimate=pl.CostEstimate(flops=0, bytes_accessed=200 << 20, transcendentals=0),
        name="front",
    )(tokens, cot, table, masters, tile_row)


def back_kernel(slots, devices, *refs):
    refs = list(refs)
    take = lambda number: [refs.pop(0) for _ in range(number)]
    dw, dw_own, own_land, dw_attn, attn_side, out, back, tokens, cot, bias, vec = take(11)
    slab, result, grad_tokens, reduced = take(4)
    dw_land, z_send, z_land, attn_send, attn_land, block, attn_sum = take(7)
    core_land, along_send, along_land, vec_land, vec_send = take(5)
    send_sems, recv_sems, local_sems = take(3)
    me, column = lax.axis_index("dp"), lax.axis_index("mlp")
    replicas = devices // 2
    links = Links(send_sems, recv_sems)
    rows = slots * TILE
    rows_ff, rows_attn = 64 * TILE // replicas, 16 * TILE // replicas
    chunks = 4
    size = rows_ff // chunks
    greet(
        me,
        column,
        [1] + [at << 1 for at in range(1, replicas)],
        [1, 2, 3],
    )
    for bit in range(4):
        total = dw_attn[0, bit].astype(F32)
        for at in range(1, replicas):
            total = total + attn_side[at - 1, bit].astype(F32)
        if bit == 0:
            attn_sum[...] = total
        else:
            attn_send[bit - 1] = total.astype(BF16)
    attn_came = [
        links.send(attn_send.at[bit - 1], attn_land.at[bit - 1], {"mlp": flip(column, bit)})
        for bit in (1, 2, 3)
    ]
    dw_came = []
    for chunk in range(chunks):
        piece = pl.ds(chunk * size, size)
        dw_came.append(
            [
                links.send(dw.at[at, piece, :], dw_land.at[at - 1, piece, :], {"dp": flip(me, at << 1)})
                for at in range(1, replicas)
            ]
        )
    core_came = []
    for number, source in ((1, back), (0, out)):
        for at in (3, 1):
            core_came.append(
                links.send(source.at[at], core_land.at[number, at // 2], {"dp": flip(me, 1)})
            )
    masks = [1 << i for i in range(devices.bit_length() - 1)]
    hops = [("dp", mask) for mask in masks] + [("mlp", 1), ("mlp", 2)]
    vec_send[0] = vec[...]
    state = {"hop": 0, "entry": None}

    def vec_step():
        hop = state["hop"]
        if hop > len(hops):
            return
        if state["entry"] is not None:
            links.arrived(state["entry"])
            value = vec_send[hop - 1] + vec_land[hop - 1]
            if hop == len(hops):
                reduced[...] = value
            else:
                vec_send[hop] = value
        if hop < len(hops):
            axis, mask = hops[hop]
            own = me if axis == "dp" else column
            state["entry"] = links.send(
                vec_send.at[hop], vec_land.at[hop], {axis: flip(own, mask)}
            )
        state["hop"] = hop + 1

    vec_step()
    step_rows = 128
    length = tokens.shape[0]

    def by_rows(function):
        def body(step, carry):
            function(pl.ds(pl.multiple_of(step * step_rows, step_rows), step_rows))
            return carry

        lax.fori_loop(0, length // step_rows, body, 0)

    along_came = {}
    for place, (number, source) in enumerate(((1, back), (0, out))):
        links.arrived(core_came[2 * place])

        def add(where, number=number, source=source):
            along_send[number, where, :] = (
                source[2, where, :].astype(F32) + core_land[number, 1, where, :].astype(F32)
            ).astype(BF16)

        by_rows(add)
        along_came[number] = links.send(
            along_send.at[number], along_land.at[number], {"mlp": flip(column, 1)}
        )
    vec_step()
    local_copies = []
    spreads = []

    def publish(first, count):
        backward = len(spreads) % 2 == 1
        spread = Spread(links, slab, me, devices, rows, first, count, backward)
        source = block.at[pl.ds(first, count), :]
        spread.forward(0, 0, source)
        copy = pltpu.make_async_copy(source, spread.part(0), local_sems.at[len(spreads)])
        copy.start()
        local_copies.append(copy)
        spreads.append(spread)

    def add_chunk(chunk):
        piece = slice(chunk * size, (chunk + 1) * size)
        for entry in dw_came[chunk]:
            links.arrived(entry)
        total = dw[0, piece, :].astype(F32)
        for at in range(1, replicas):
            total = total + dw_land[at - 1, piece, :].astype(F32)
        z_send[piece, :] = total.astype(BF16)
        where = pl.ds(chunk * size, size)
        return links.send(z_send.at[where, :], z_land.at[where, :], {"mlp": flip(column, 2)})

    z_came = [add_chunk(0)]
    for entry in attn_came:
        links.arrived(entry)
    block[rows_ff : rows_ff + rows_attn, :] = (
        attn_sum[...] + attn_land[1].astype(F32)
    ).astype(BF16)
    publish(rows_ff, rows_attn)
    block[rows_ff + rows_attn : rows, :] = (
        attn_land[0].astype(F32) + attn_land[2].astype(F32)
    ).astype(BF16)
    publish(rows_ff + rows_attn, rows_attn)
    vec_step()
    for chunk in range(1, chunks):
        z_came.append(add_chunk(chunk))
    vec_step()
    for spread in spreads[:2]:
        spread.relay()
    for chunk in range(chunks):
        links.arrived(z_came[chunk])
        piece = slice(chunk * size, (chunk + 1) * size)
        total = z_land[piece, :].astype(F32) + dw_own[0, piece, :].astype(F32)
        for at in range(1, replicas):
            total = total + own_land[at - 1, piece, :].astype(F32)
        block[piece, :] = total.astype(BF16)
        publish(chunk * size, size)
        vec_step()
        if chunk > 0:
            spreads[1 + chunk].relay()
    spreads[1 + chunks].relay()

    links.arrived(core_came[1])
    links.arrived(along_came[1])

    def finish_back(where):
        value = tokens[where, :]
        value = value - jnp.mean(value, axis=-1, keepdims=True)
        inverse = lax.rsqrt(jnp.mean(value * value, axis=-1, keepdims=True) + eps_norm)
        hat = value * inverse
        grad = back[0, where, :].astype(F32) + core_land[1, 0, where, :].astype(F32)
        grad = grad + along_land[1, where, :].astype(F32)
        grad_tokens[where, :] = cot[where, :] + inverse * (
            grad
            - jnp.mean(grad, axis=-1, keepdims=True)
            - hat * jnp.mean(grad * hat, axis=-1, keepdims=True)
        )

    by_rows(finish_back)
    links.arrived(core_came[3])
    links.arrived(along_came[0])

    def finish_out(where):
        value = out[0, where, :].astype(F32) + core_land[0, 0, where, :].astype(F32)
        value = value + along_land[0, where, :].astype(F32)
        result[where, :] = tokens[where, :] + (value + (bias[7:8, :] + bias[8:9, :]))

    by_rows(finish_out)
    while state["hop"] <= len(hops):
        vec_step()
    for copy in local_copies:
        copy.wait()
    links.finish()


def send_back(dw, own, attn, out, back, tokens, cot, vectors, vec, slots):
    length, width = tokens.shape
    devices = lax.axis_size("dp")
    replicas = devices // 2
    rows_ff, rows_attn = 64 * TILE // replicas, 16 * TILE // replicas
    rows = slots * TILE
    pieces = 6
    hops = devices.bit_length() + 1
    count = 3 + 4 * (replicas - 1) + 4 + 2 + hops + 4 + pieces * (2 * replicas - 1)
    return pl.pallas_call(
        functools.partial(back_kernel, slots, devices),
        out_shape=[
            jax.ShapeDtypeStruct((devices * rows, LANES), BF16),
            jax.ShapeDtypeStruct((length, width), F32),
            jax.ShapeDtypeStruct((length, width), F32),
            jax.ShapeDtypeStruct(vec.shape, F32),
        ],
        in_specs=[VMEM] * 11,
        out_specs=[ANY] + [VMEM] * 3,
        scratch_shapes=[
            pltpu.VMEM((replicas - 1, rows_ff, LANES), BF16),
            pltpu.VMEM((rows_ff, LANES), BF16),
            pltpu.VMEM((rows_ff, LANES), BF16),
            pltpu.VMEM((3, rows_attn, LANES), BF16),
            pltpu.VMEM((3, rows_attn, LANES), BF16),
            pltpu.VMEM((rows, LANES), BF16),
            pltpu.VMEM((rows_attn, LANES), F32),
            pltpu.VMEM((2, 2, length, width), BF16),
            pltpu.VMEM((2, length, width), BF16),
            pltpu.VMEM((2, length, width), BF16),
            pltpu.VMEM((hops,) + vec.shape, F32),
            pltpu.VMEM((hops,) + vec.shape, F32),
            pltpu.SemaphoreType.DMA((count,)),
            pltpu.SemaphoreType.DMA((count,)),
            pltpu.SemaphoreType.DMA((pieces,)),
        ],
        compiler_params=pltpu.CompilerParams(
            vmem_limit_bytes=60 << 20, collective_id=1, has_side_effects=True
        ),
        cost_estimate=pl.CostEstimate(flops=0, bytes_accessed=200 << 20, transcendentals=0),
        name="send_back",
    )(dw, *own, *attn, out, back, tokens, cot, vectors, vec)


def erf_f32(value):
    value = jnp.clip(value, -3.832506856900711, 3.832506856900711)
    square = value * value
    top = jnp.full_like(square, 0.00022905065861350646)
    for coeff in (
        0.0034082910107109506,
        0.050955695062380861,
        0.18520832239976145,
        1.128379143519084,
    ):
        top = top * square + coeff
    low = jnp.full_like(square, -1.1791602954361697e-7)
    for coeff in (
        0.000023547966471313185,
        0.0010179625278914885,
        0.014070470171167667,
        0.11098505178285362,
        0.49746925110067538,
        1.0,
    ):
        low = low * square + coeff
    return value * top / low


def ff_kernel(count, has_acc, replicas, *refs):
    refs = list(refs)
    take = lambda number: [refs.pop(0) for _ in range(number)]
    norm_ref, bias_ref, side_ref = take(3)
    h_ref, c_ref = take(2)
    part_refs = take(count)
    acc_refs = take(2) if has_acc else None
    out_ref, gd_ref, dw_ref, vec_ref, hid_ref, land_ref = take(6)
    h_all, c_all, tiles, up, down, up_acc, down_acc, sems, send_sems, recv_sems = take(10)
    quarter = lax.axis_index("dp") // 2
    if has_acc:
        moves = [
            (side_ref.at[at], land_ref.at[at - 1], "dp", at << 1) for at in range(1, replicas)
        ]
    else:
        moves = [(side_ref, land_ref, "mlp", 2)]
    links = start_side(moves, send_sems, recv_sems)
    copies = []
    for number in range(4):
        copies.append(pltpu.make_async_copy(h_ref.at[number], h_all.at[number], sems.at[number]))
        copies.append(
            pltpu.make_async_copy(c_ref.at[number], c_all.at[number], sems.at[4 + number])
        )
    for copy in copies:
        copy.start()
    rows_part = part_refs[0].shape[0]
    for at in range(replicas if count > 1 else 1):
        where = differ(at, quarter, replicas) if count > 1 else 0
        tiles[pl.ds(pl.multiple_of(where * rows_part, TILE), rows_part), :] = (
            part_refs[0][...] if at == 0 else part_refs[1][at - 1]
        )
    for at in range(32):
        up[(at // 4) * TILE : (at // 4 + 1) * TILE, (at % 4) * TILE : (at % 4 + 1) * TILE] = tiles[
            at * TILE : (at + 1) * TILE, :
        ]
        down[(at // 8) * TILE : (at // 8 + 1) * TILE, (at % 8) * TILE : (at % 8 + 1) * TILE] = (
            tiles[(32 + at) * TILE : (33 + at) * TILE, :]
        )
    up_acc[...] = jnp.zeros_like(up_acc)
    down_acc[...] = jnp.zeros_like(down_acc)
    vec_ref[...] = jnp.zeros_like(vec_ref)
    hid_ref[...] = jnp.zeros_like(hid_ref)
    for copy in copies:
        copy.wait()

    def body(at, carry):
        hat = h_all[at].astype(F32)
        normed = (hat * norm_ref[2:3, :] + norm_ref[3:4, :]).astype(BF16)
        cot = c_all[at]
        pre = dot_nn(normed, up[...]) + bias_ref[...]
        cdf = 0.5 + 0.5 * erf_f32(pre * 0.7071067811865476)
        hidden = (pre * cdf).astype(BF16)
        grad = dot_nt(cot, down[...])
        grad = grad * (cdf + pre * (jnp.exp(-0.5 * pre * pre) * 0.3989422804014327))
        grad = grad.astype(BF16)
        hid_ref[...] += jnp.sum(grad.astype(F32), axis=0, keepdims=True)
        out = dot_nn(hidden, down[...])
        back = dot_nt(grad, up[...])
        vec_ref[0:1, :] += jnp.sum(back * hat, axis=0, keepdims=True)
        vec_ref[1:2, :] += jnp.sum(back, axis=0, keepdims=True)
        back = back * norm_ref[2:3, :]
        if acc_refs is not None:
            out = out + acc_refs[0][at].astype(F32)
            back = back + acc_refs[1][at].astype(F32)
        out_ref[at] = out.astype(BF16)
        gd_ref[at] = back.astype(BF16)
        up_acc[...] += dot_tn(normed, grad)
        down_acc[...] += dot_tn(hidden, cot)
        return carry

    lax.fori_loop(0, 4, body, 0)
    rows_out = dw_ref.shape[1]
    per = rows_out // TILE
    for at in range(64):
        if at < 32:
            tile = up_acc[
                (at // 4) * TILE : (at // 4 + 1) * TILE, (at % 4) * TILE : (at % 4 + 1) * TILE
            ]
        else:
            low = at - 32
            tile = down_acc[
                (low // 8) * TILE : (low // 8 + 1) * TILE, (low % 8) * TILE : (low % 8 + 1) * TILE
            ]
        dw_ref[
            differ(at // per, quarter, replicas), (at % per) * TILE : (at % per + 1) * TILE, :
        ] = tile.astype(BF16)
    links.finish()


def feed_forward(vectors, bias, side, hats, cots, parts, acc, replicas):
    length, width = hats.shape[1:]
    hidden = 4 * TILE
    rows_out = 64 * TILE // replicas
    acc_list = list(acc) if acc is not None else []
    land = side.shape if acc is None else (replicas - 1,) + side.shape[1:]
    moves = 1 if acc is None else replicas - 1
    return pl.pallas_call(
        functools.partial(ff_kernel, len(parts), acc is not None, replicas),
        out_shape=[
            jax.ShapeDtypeStruct((4, length, width), BF16),
            jax.ShapeDtypeStruct((4, length, width), BF16),
            jax.ShapeDtypeStruct((replicas, rows_out, LANES), BF16),
            jax.ShapeDtypeStruct((2, width), F32),
            jax.ShapeDtypeStruct((1, hidden), F32),
            jax.ShapeDtypeStruct(land, BF16),
        ],
        in_specs=[VMEM, VMEM] + [ANY] * 3 + [VMEM] * (len(parts) + len(acc_list)),
        out_specs=[VMEM] * 5 + [ANY],
        scratch_shapes=[
            pltpu.VMEM((4, length, width), BF16),
            pltpu.VMEM((4, length, width), BF16),
            pltpu.VMEM((64 * TILE, LANES), BF16),
            pltpu.VMEM((width, hidden), BF16),
            pltpu.VMEM((hidden, width), BF16),
            pltpu.VMEM((width, hidden), F32),
            pltpu.VMEM((hidden, width), F32),
            pltpu.SemaphoreType.DMA((8,)),
        ]
        + side_shapes(moves),
        compiler_params=pltpu.CompilerParams(
            vmem_limit_bytes=60 << 20,
            collective_id=2 if acc is None else 3,
            has_side_effects=True,
        ),
        cost_estimate=pl.CostEstimate(
            flops=12 * 4 * length * width * hidden, bytes_accessed=20 << 20, transcendentals=0
        ),
        name="feed_forward",
    )(vectors, bias, side, hats, cots, *parts, *acc_list)


def attn_kernel(count, replicas, *refs):
    refs = list(refs)
    take = lambda number: [refs.pop(0) for _ in range(number)]
    norm_ref, bias_ref, spread_ref, side_ff, side_dw = take(5)
    tab_ref, h_ref, c_ref, own_ref, part_ref = take(5)
    acc_refs = take(2)
    out_ref, gd_ref, dw_ref, vec_ref, sum_ref, land_ff, land_dw = take(7)
    h_all, c_all, tiles, w_in, w_out, in_acc, out_acc = take(7)
    q_all, k_all, v_all, g_all, o_all, dq_all, dk_all, dv_all, sems = take(9)
    send_sems, recv_sems = take(2)
    me, column = lax.axis_index("dp"), lax.axis_index("mlp")
    quarter = me // 2
    moves = []
    for at in range(1, replicas):
        moves.append((side_ff, land_ff.at[at - 1], "dp", at << 1))
        moves.append((side_dw.at[at], land_dw.at[at - 1], "dp", at << 1))
    links = start_side(moves, send_sems, recv_sems)
    copies = []
    for number in range(4):
        copies.append(pltpu.make_async_copy(h_ref.at[number], h_all.at[number], sems.at[number]))
        copies.append(
            pltpu.make_async_copy(c_ref.at[number], c_all.at[number], sems.at[4 + number])
        )
    for copy in copies:
        copy.start()
    tiles[column] = own_ref[...]
    rows_part = 16 * TILE // count
    for at in range(count):
        first = pl.multiple_of(differ(at, quarter, replicas) * rows_part, rows_part)
        for bit in (1, 2, 3):
            tiles[flip(column, bit), pl.ds(first, rows_part), :] = part_ref[
                at, (bit - 1) * rows_part : bit * rows_part, :
            ]
    for matrix in range(3):
        for at in range(16):
            w_in[
                (at // 2) * TILE : (at // 2 + 1) * TILE,
                (2 * matrix + at % 2) * TILE : (2 * matrix + at % 2 + 1) * TILE,
            ] = tiles[matrix, at * TILE : (at + 1) * TILE, :]
    for at in range(16):
        w_out[(at // 8) * TILE : (at // 8 + 1) * TILE, (at % 8) * TILE : (at % 8 + 1) * TILE] = (
            tiles[3, at * TILE : (at + 1) * TILE, :]
        )
    in_acc[...] = jnp.zeros_like(in_acc)
    out_acc[...] = jnp.zeros_like(out_acc)
    vec_ref[...] = jnp.zeros_like(vec_ref)
    sum_ref[...] = jnp.zeros_like(sum_ref)
    for copy in copies:
        copy.wait()
    length = h_all.shape[1]
    wide = 4 * HDIM
    block = 256
    half = ROT // 2
    lane = lax.broadcasted_iota(jnp.int32, (1, LANES), 1) % (2 * HDIM)
    keep_low = lane < HDIM
    scale = HDIM ** (-0.5)

    def body(at, carry):
        hat = h_all[at].astype(F32)
        normed = (hat * norm_ref[0:1, :] + norm_ref[1:2, :]).astype(BF16)
        cot = c_all[at]
        table = precise(tab_ref[at], spread_ref[...], 0, 0)
        within = lane % HDIM
        cos_w = table[:, 0:LANES] + (within >= ROT).astype(F32)
        sin_a = table[:, LANES : 2 * LANES]
        sin_b = table[:, 2 * LANES : 3 * LANES]
        proj = dot_nn(normed, w_in[...]) + bias_ref[...]
        g_all[...] = dot_nt(cot, w_out[...]).astype(BF16)
        for pair in range(2):
            cols = slice(pair * LANES, (pair + 1) * LANES)
            query = proj[:, pair * LANES : (pair + 1) * LANES]
            key = proj[:, wide + pair * LANES : wide + (pair + 1) * LANES]

            def turn(value):
                return (
                    value * cos_w
                    - pltpu.roll(value, LANES - half, 1) * sin_a
                    + pltpu.roll(value, half, 1) * sin_b
                )

            q_all[:, cols] = (turn(query).astype(BF16) * scale).astype(BF16)
            k_all[:, cols] = turn(key).astype(BF16)
            v_all[:, cols] = proj[:, 2 * wide + pair * LANES : 2 * wide + (pair + 1) * LANES].astype(
                BF16
            )
        dk_all[...] = jnp.zeros_like(dk_all)
        dv_all[...] = jnp.zeros_like(dv_all)
        for pair in range(2):
            cols = slice(pair * LANES, (pair + 1) * LANES)
            for first in range(0, length, block):
                rows = slice(first, first + block)
                keys = slice(0, first + block)
                out_rows = None
                dq_rows = None
                for head in range(2):
                    mask = keep_low if head == 0 else jnp.logical_not(keep_low)
                    zero = jnp.zeros((), BF16)
                    query = jnp.where(mask, q_all[rows, cols], zero)
                    grad = jnp.where(mask, g_all[rows, cols], zero)
                    key = jnp.where(mask, k_all[keys, cols], zero)
                    value = jnp.where(mask, v_all[keys, cols], zero)
                    scores = dot_nt(query, key)
                    row_at = first + lax.broadcasted_iota(jnp.int32, scores.shape, 0)
                    col_at = lax.broadcasted_iota(jnp.int32, scores.shape, 1)
                    scores = jnp.where(col_at <= row_at, scores, -1e30)
                    peak = jnp.max(scores, axis=-1, keepdims=True)
                    raised = jnp.exp(scores - peak)
                    prob = raised * (1.0 / jnp.sum(raised, axis=-1, keepdims=True))
                    prob_low = prob.astype(BF16)
                    piece = dot_nn(prob_low, value)
                    out_rows = piece if out_rows is None else out_rows + piece
                    grad_prob = dot_nt(grad, value)
                    delta = jnp.sum(prob * grad_prob, axis=-1, keepdims=True)
                    grad_scores = (prob * (grad_prob - delta)).astype(BF16)
                    piece = dot_nn(grad_scores, key)
                    dq_rows = piece if dq_rows is None else dq_rows + piece
                    dk_all[keys, cols] += dot_tn(grad_scores, query)
                    dv_all[keys, cols] += dot_tn(prob_low, grad)
                o_all[rows, cols] = out_rows.astype(BF16)
                dq_all[rows, cols] = dq_rows * scale

        def turn_back(value):
            return (
                value * cos_w
                + pltpu.roll(value, LANES - half, 1) * sin_a
                - pltpu.roll(value, half, 1) * sin_b
            ).astype(BF16)

        pieces = [turn_back(dq_all[:, 0:LANES]), turn_back(dq_all[:, LANES : 2 * LANES])]
        pieces += [turn_back(dk_all[:, 0:LANES]), turn_back(dk_all[:, LANES : 2 * LANES])]
        pieces += [dv_all[...].astype(BF16)]
        grads = jnp.concatenate(pieces, axis=1)
        sum_ref[...] += jnp.sum(grads.astype(F32), axis=0, keepdims=True)
        out = dot_nn(o_all[...], w_out[...]) + acc_refs[0][at].astype(F32)
        out_ref[at] = out.astype(BF16)
        back = dot_nt(grads, w_in[...])
        vec_ref[0:1, :] += jnp.sum(back * hat, axis=0, keepdims=True)
        vec_ref[1:2, :] += jnp.sum(back, axis=0, keepdims=True)
        back = back * norm_ref[0:1, :] + acc_refs[1][at].astype(F32)
        gd_ref[at] = back.astype(BF16)
        in_acc[...] += dot_tn(normed, grads)
        out_acc[...] += dot_tn(o_all[...], cot)
        return carry

    lax.fori_loop(0, 4, body, 0)
    rows_out = dw_ref.shape[2]
    size = min(TILE, rows_out)
    for matrix in range(4):
        for at in range(16):
            for piece in range(TILE // size):
                row = at * TILE + piece * size
                if matrix < 3:
                    top, left = (at // 2) * TILE, (2 * matrix + at % 2) * TILE
                    tile = in_acc[top + piece * size : top + (piece + 1) * size, left : left + TILE]
                else:
                    top, left = (at // 8) * TILE, (at % 8) * TILE
                    tile = out_acc[
                        top + piece * size : top + (piece + 1) * size, left : left + TILE
                    ]
                inner = row % rows_out
                dw_ref[
                    differ(row // rows_out, quarter, replicas),
                    flip(column, matrix),
                    inner : inner + size,
                    :,
                ] = tile.astype(BF16)
    links.finish()


def attention(vectors, bias, spread, side_ff, side_dw, tables, hats, cots, own, parts, acc, replicas):
    length, width = hats.shape[1:]
    wide = 4 * HDIM
    rows_out = 16 * TILE // replicas
    return pl.pallas_call(
        functools.partial(attn_kernel, replicas, replicas),
        out_shape=[
            jax.ShapeDtypeStruct((4, length, width), BF16),
            jax.ShapeDtypeStruct((4, length, width), BF16),
            jax.ShapeDtypeStruct((replicas, 4, rows_out, LANES), BF16),
            jax.ShapeDtypeStruct((2, width), F32),
            jax.ShapeDtypeStruct((1, 3 * wide), F32),
            jax.ShapeDtypeStruct((replicas - 1,) + side_ff.shape, BF16),
            jax.ShapeDtypeStruct((replicas - 1,) + side_dw.shape[1:], BF16),
        ],
        in_specs=[VMEM, VMEM, VMEM, ANY, ANY, VMEM, ANY, ANY] + [VMEM] * 4,
        out_specs=[VMEM] * 5 + [ANY] * 2,
        scratch_shapes=[
            pltpu.VMEM((4, length, width), BF16),
            pltpu.VMEM((4, length, width), BF16),
            pltpu.VMEM((4, 16 * TILE, LANES), BF16),
            pltpu.VMEM((width, 3 * wide), BF16),
            pltpu.VMEM((wide, width), BF16),
            pltpu.VMEM((width, 3 * wide), F32),
            pltpu.VMEM((wide, width), F32),
            pltpu.VMEM((length, wide), BF16),
            pltpu.VMEM((length, wide), BF16),
            pltpu.VMEM((length, wide), BF16),
            pltpu.VMEM((length, wide), BF16),
            pltpu.VMEM((length, wide), BF16),
            pltpu.VMEM((length, wide), F32),
            pltpu.VMEM((length, wide), F32),
            pltpu.VMEM((length, wide), F32),
            pltpu.SemaphoreType.DMA((8,)),
        ]
        + side_shapes(2 * (replicas - 1)),
        compiler_params=pltpu.CompilerParams(
            vmem_limit_bytes=60 << 20, collective_id=4, has_side_effects=True
        ),
        cost_estimate=pl.CostEstimate(
            flops=30 * 10**9, bytes_accessed=20 << 20, transcendentals=0
        ),
        name="attention",
    )(vectors, bias, spread, side_ff, side_dw, tables, hats, cots, own, parts, *acc)


def soap_kernel(slots, replicas, per_step, *refs):
    refs = list(refs)
    take = lambda number: [refs.pop(0) for _ in range(number)]
    place_ref, owner_ref, slab = take(3)
    left_ref, right_ref, first_ref, second_ref, master_ref, ema_ref = take(6)
    grad_ref, first_out, second_out, master_out, copy_out, ema_out = take(6)
    mine, inverse, sem = take(3)
    me, column = place_ref[0], place_ref[1]
    step = pl.program_id(0)
    bias_fix = 1.0 - 0.5**STEP
    rows_ff = 64 * TILE // replicas
    rows_attn = 16 * TILE // replicas
    rows_all = slots * TILE
    size = min(TILE, rows_attn)

    @pl.when(step == 0)
    def _():
        def note(unit, carry):
            inverse[owner_ref[unit]] = unit
            return carry

        lax.fori_loop(0, owner_ref.shape[0], note, 0)

        def fetch(number, carry):
            unit = inverse[me * slots + number]
            row, col = (unit % 64) // 8, unit % 8
            by_rows = column == 3
            rank = jnp.where(by_rows, row // 2, col // 2)
            attn_place = jnp.where(by_rows, (row % 2) * 8 + col, row * 2 + col % 2)
            up_place = row * 4 + col % 4
            down_place = 32 + (row % 4) * 8 + col
            is_attn, is_up = unit < 64, unit < 128
            core = jnp.where(is_attn, rank % 2, jnp.where(is_up, col // 4, row // 4))
            other = ((rank // 2) != (column % 2)).astype(jnp.int32)
            for piece in range(TILE // size):
                attn_row = attn_place * TILE + piece * size
                ff_row = jnp.where(is_up, up_place, down_place) * TILE + piece * size
                holder = jnp.where(is_attn, attn_row // rows_attn, ff_row // rows_ff)
                inner = jnp.where(
                    is_attn, rows_ff + other * rows_attn + attn_row % rows_attn, ff_row % rows_ff
                )
                start = ((holder * 2 + core) ^ me) * rows_all + inner
                pltpu.make_async_copy(
                    slab.at[pl.ds(pl.multiple_of(start, size), size), :],
                    mine.at[number, pl.ds(piece * size, size), :],
                    sem,
                ).start()
            return carry

        lax.fori_loop(0, slots, fetch, 0)
        pltpu.make_async_copy(mine, mine, sem).wait()

    for number in range(per_step):
        grad = mine[step * per_step + number].astype(F32)
        left, right = left_ref[number], right_ref[number]
        grad_ref[number] = grad
        turned = precise(precise(left, grad, 0, 0), right, 1, 0)
        first = 0.5 * first_ref[number] + 0.5 * turned
        second = 0.5 * second_ref[number] + 0.5 * turned * turned
        first_out[number] = first
        second_out[number] = second
        scaled = first / bias_fix / (jnp.sqrt(second / bias_fix) + eps_adam)
        back = precise(precise(left, scaled, 1, 0), right, 1, 1)
        master = master_ref[number] - lr_matrix * back
        master_out[number] = master
        copy_out[number] = master.astype(BF16)
        ema_out[number] = ema_keep * ema_ref[number] + (1.0 - ema_keep) * master


def soap(place, owner_row, slab, state, replicas):
    slots = state[0].shape[0]
    per_step = 4 if slots % 4 == 0 else 1
    spec = pl.BlockSpec((per_step, TILE, TILE), lambda i: (i, 0, 0))
    shape = (slots, TILE, TILE)
    return pl.pallas_call(
        functools.partial(soap_kernel, slots, replicas, per_step),
        grid=(slots // per_step,),
        out_shape=[jax.ShapeDtypeStruct(shape, F32)] * 4
        + [jax.ShapeDtypeStruct(shape, BF16), jax.ShapeDtypeStruct(shape, F32)],
        in_specs=[SMEM, SMEM, ANY] + [spec] * 6,
        out_specs=[spec] * 6,
        scratch_shapes=[
            pltpu.VMEM(shape, BF16),
            pltpu.SMEM((owner_row.shape[0],), jnp.int32),
            pltpu.SemaphoreType.DMA,
        ],
        compiler_params=pltpu.CompilerParams(vmem_limit_bytes=32 << 20),
        cost_estimate=pl.CostEstimate(
            flops=24 * slots * 2 * TILE**3, bytes_accessed=20 << 20, transcendentals=0
        ),
        name="soap",
    )(place, owner_row, slab, *state)


def adam_step(grad, first, second, param):
    bias_fix = 1.0 - 0.5**STEP
    first_new = 0.5 * first + 0.5 * grad
    second_new = 0.5 * second + 0.5 * grad * grad
    return (
        first_new,
        second_new,
        param - lr_vector * (first_new / bias_fix) / (jnp.sqrt(second_new / bias_fix) + eps_adam),
    )


def spread_table():
    lane = jnp.arange(LANES, dtype=jnp.int32) % HDIM
    row = jnp.arange(ROT, dtype=jnp.int32)[:, None]
    half = ROT // 2
    cos_part = (lane < ROT) & (row == lane % half)
    sin_first = (lane < half) & (row == half + lane)
    sin_second = (lane >= half) & (lane < ROT) & (row == lane)
    return jnp.concatenate([cos_part, sin_first, sin_second], axis=1).astype(F32)


def local(
    tokens,
    cotangent,
    positions,
    owners,
    masters,
    basis_left,
    basis_right,
    moment1,
    moment2,
    ema,
    vectors,
    vector_moment1,
    vector_moment2,
    hidden_bias,
    hidden_moment1,
    hidden_moment2,
):
    length, width = tokens.shape
    slots = masters.shape[1]
    me = lax.axis_index("dp")
    column = lax.axis_index("mlp")
    replicas = lax.axis_size("dp") // 2
    core, low = me % 2, column % 2
    rank = 2 * low + core
    place = jnp.stack([me, column, me // 2]).astype(jnp.int32)
    owner_row = owners[0]

    inverse_freq = 10000.0 ** (-(jnp.arange(ROT // 2, dtype=F32) * 2.0) / ROT)
    angles = inverse_freq[:, None] * positions.astype(F32)[None, :]
    table = jnp.concatenate([jnp.cos(angles), jnp.sin(angles)], axis=0)
    hats, cots, tables, attn_parts, own_attn, own_ff, send_ff = front(
        tokens, cotangent, table, masters[0], (owner_row // slots ^ me) * slots + owner_row % slots
    )

    hidden = FF // (2 * GROUP)
    start_own = column * (2 * hidden) + core * hidden
    start_other = (column ^ 2) * (2 * hidden) + core * hidden
    bias_own = lax.dynamic_slice_in_dim(hidden_bias, start_own, hidden, 0)[None]
    bias_other = lax.dynamic_slice_in_dim(hidden_bias, start_other, hidden, 0)[None]
    wide = width // GROUP
    bias_qkv = lax.dynamic_slice(vectors, (4, rank * wide), (3, wide)).reshape(1, 3 * wide)

    out, back, dw_own, vec_own, hid_own, other_ff = feed_forward(
        vectors, bias_own, send_ff, hats, cots, [own_ff], None, replicas
    )
    out, back, dw_attn, vec_attn, sums, ff_land, own_land = attention(
        vectors,
        bias_qkv,
        spread_table(),
        other_ff,
        dw_own,
        tables,
        hats,
        cots,
        own_attn,
        attn_parts,
        (out, back),
        replicas,
    )
    out, back, dw_other, vec_other, hid_other, attn_side = feed_forward(
        vectors, bias_other, dw_attn, hats, cots, [other_ff, ff_land], (out, back), replicas
    )
    grad_bias_out = jnp.sum(cotangent.astype(BF16).astype(F32), axis=0)
    sums = lax.dynamic_update_slice(
        jnp.zeros((3, width), F32), sums.reshape(3, wide), (0, rank * wide)
    )
    hidden_part = lax.dynamic_update_slice_in_dim(
        jnp.zeros((FF,), F32), hid_own[0], start_own, 0
    )
    hidden_part = lax.dynamic_update_slice_in_dim(hidden_part, hid_other[0], start_other, 0)
    vector_part = jnp.concatenate(
        [
            vec_attn,
            vec_own + vec_other,
            sums,
            grad_bias_out[None],
            hidden_part.reshape(-1, width),
        ],
        axis=0,
    )
    slab, result, grad_tokens, reduced = send_back(
        dw_other,
        (dw_own, own_land),
        (dw_attn, attn_side),
        out,
        back,
        tokens,
        cotangent,
        vectors,
        vector_part,
        slots,
    )
    state = [item[0] for item in (basis_left, basis_right, moment1, moment2, masters, ema)]
    own_grad, first_new, second_new, master_new, weight_copy, ema_new = soap(
        place, owner_row, slab, state, replicas
    )
    vector_grad = jnp.concatenate([reduced[:8], reduced[7:8]], axis=0)
    hidden_grad = reduced[8:].reshape(FF)
    vec_first, vec_second, vectors_new = adam_step(
        vector_grad, vector_moment1, vector_moment2, vectors
    )
    hid_first, hid_second, hidden_new = adam_step(
        hidden_grad, hidden_moment1, hidden_moment2, hidden_bias
    )
    return (
        result,
        grad_tokens,
        own_grad[None],
        first_new[None],
        second_new[None],
        master_new[None],
        weight_copy[None],
        ema_new[None],
        vector_grad,
        vec_first,
        vec_second,
        vectors_new,
        hidden_grad,
        hid_first,
        hid_second,
        hidden_new,
    )


def solution(mesh):
    split = P(("dp", "mlp"), None)
    tiled = P("mlp", "dp", None, None)
    return jax.shard_map(
        local,
        mesh=mesh,
        in_specs=(split, split, P(("dp", "mlp")), P("mlp", None)) + (tiled,) * 6 + (P(),) * 6,
        out_specs=(split, split) + (tiled,) * 6 + (P(),) * 8,
        check_vma=False,
    )
```

profile of v0, /device:TPU:7, one launch (start us, length us, event | category | flops | bytes accessed | tf_op | source)
XLA Modules:
  0.0 367.2 jit_solution(8588310231860888844)
XLA Ops:
  0.7 1.4 fusion.9
  3.6 1.6 copy-done
  5.2 1.6 copy-done.2
  6.8 1.4 copy-done.4
  8.2 76.4 %front.1 = (bf16[4,512,1024]{2,1,0:T(8,128)(2,1)S(1)}, bf16[4,512,1024]{2,1,0:T(8,128)(2,1)S(1)}, f32[4,16,512]{2,1,0:T(8,128)S(1)}, bf16[4,1536,128]{2,1,0:T(8,...) custom-call(f32[512,1024]{1,0:T(8,128)S(1)} %copy-done.2, ...), custom_call_target="tpu_custom_call" | custom-call | bytes 209715200 | tf_op jit(solution)/shard_map/front/pallas_call | solution.py:291
  84.6 2.0 copy-done.12
  86.5 2.0 copy-done.13
  88.6 1.3 copy-done.14
  89.9 1.1 copy-done.15
  91.0 0.8 copy-done.16
  91.8 0.8 copy-done.17
  93.3 31.0 %feed_forward.2 = (bf16[4,512,1024]{2,1,0:T(8,128)(2,1)}, bf16[4,512,1024]{2,1,0:T(8,128)(2,1)}, bf16[4,2048,128]{2,1,0:T(8,128)(2,1)}, f32[2,1024]{1,0:T(2,128)...) custom-call(f32[9,1024]{1,0:T(8,128)} %refs_9_.1, f32[1,512]{1,0:T(1,128)} %bitcast.44, bf16[2048,128]{1,0:T(8,128)(2,1)} %copy-done.17, ...), custom_call_target="tpu_custom_call" | custom-call | flops 12884901888 | bytes 20971520 | tf_op jit(solution)/shard_map/feed_forward/pallas_call | solution.py:669
  124.3 0.8 dynamic-slice_bitcast_fusion
  126.3 56.6 %attention.1 = (bf16[4,512,1024]{2,1,0:T(8,128)(2,1)}, bf16[4,512,1024]{2,1,0:T(8,128)(2,1)}, bf16[4,4,512,128]{3,2,1,0:T(8,128)(2,1)}, f32[2,1024]{1,0:T(2,128)...) custom-call(f32[9,1024]{1,0:T(8,128)} %refs_9_.1, f32[1,768]{1,0:T(1,128)} %bitcast.40, ...), custom_call_target="tpu_custom_call" | custom-call | flops 30000001024 | bytes 20971520 | tf_op jit(solution)/shard_map/attention/pallas_call | solution.py:877
  183.0 32.4 %feed_forward.3 = (bf16[4,512,1024]{2,1,0:T(8,128)(2,1)}, bf16[4,512,1024]{2,1,0:T(8,128)(2,1)}, bf16[4,2048,128]{2,1,0:T(8,128)(2,1)}, f32[2,1024]{1,0:T(2,128)...) custom-call(f32[9,1024]{1,0:T(8,128)} %refs_9_.1, f32[1,512]{1,0:T(1,128)} %bitcast.43, ...), custom_call_target="tpu_custom_call" | custom-call | flops 12884901888 | bytes 20971520 | tf_op jit(solution)/shard_map/feed_forward/pallas_call | solution.py:669
  215.7 0.8 dynamic_update_slice.11
  216.6 0.7 add.123
  217.5 1.3 concatenate.14.refs_10_
  218.8 108.3 %send_back.1 = (bf16[24576,128]{1,0:T(8,128)(2,1)}, f32[512,1024]{1,0:T(8,128)}, f32[512,1024]{1,0:T(8,128)}, f32[12,1024]{1,0:T(8,128)}) custom-call(bf16[4,2048,128]{2,1,0:T(8,128)(2,1)} %get-tuple-element.67.refs_0_, bf16[4,2048,128]{2,1,0:T(8,128)(2,1)} %get-tuple-element.57.refs_4_.refs_1_, bf16[3,2048,128]{2,1,0:T(8,128)(2,1)} %get-tuple-element.68.refs_2_, ...), custom_call_target="tpu_custom_call" | custom-call | bytes 209715200 | tf_op jit(solution)/shard_map/send_back/pallas_call | solution.py:514
  327.2 0.8 slice.9
  327.9 0.8 slice.10
  328.7 0.7 divide_subtract_fusion
  329.5 2.8 copy-done.3
  332.3 1.4 copy-done.7
  333.7 1.4 copy-done.8
  335.1 1.4 copy-done.9
  336.5 1.4 copy-done.10
  337.9 24.2 %soap.1 = (f32[24,128,128]{2,1,0:T(8,128)}, f32[24,128,128]{2,1,0:T(8,128)}, f32[24,128,128]{2,1,0:T(8,128)}, f32[24,128,128]{2,1,0:T(8,128)}, bf16[24,128,128]{2,1,0:T(8,128)(2,1)}, /*index=5*/f32[24,128,128]{2,1,0:T(8,128)}) custom-call(s32[3]{0:T(128)S(1)} %pad_add_fusion.refs_0_, s32[192]{0:T(256)S(1)} %bitcast.38, bf16[24576,128]{1,0:T(8,128)(2,1)S(1)} %copy-done.3, ...), custom_call_target="tpu_custom_call" | custom-call | flops 2415919104 | bytes 20971520 | tf_op jit(solution)/shard_map/soap/pallas_call | solution.py:993
  362.2 0.8 slice_bitcast_fusion
  363.6 1.3 copy.41
  364.9 1.0 copy-done.19
  365.9 1.3 copy.42
  (72 shorter events, 4.7 us)
Async XLA Ops:
  3.6 1.6 copy-start
  5.2 1.6 copy-start.2
  6.8 1.4 copy-start.4
  84.6 2.0 copy-start.12
  86.5 2.0 copy-start.13
  88.6 1.3 copy-start.14
  89.9 1.1 copy-start.15
  91.0 0.8 copy-start.16
  91.8 0.8 copy-start.17
  92.6 0.7 copy-start.18
  183.0 32.5 %copy-start.30 = (f32[1,512]{1,0:T(1,128)S(1)}, f32[1,512]{1,0:T(1,128)}, u32[]{:S(2)}) copy-start(f32[1,512]{1,0:T(1,128)} %get-tuple-element.76) | copy-start | bytes 6148
  183.0 33.6 %copy-start.27 = (f32[2,1024]{1,0:T(2,128)S(1)}, f32[2,1024]{1,0:T(2,128)}, u32[]{:S(2)}) copy-start(f32[2,1024]{1,0:T(2,128)} %get-tuple-element.73) | copy-start | bytes 24580
  183.0 34.3 %copy-start.29 = (f32[1,768]{1,0:T(1,128)S(1)}, f32[1,768]{1,0:T(1,128)}, u32[]{:S(2)}) copy-start(f32[1,768]{1,0:T(1,128)} %get-tuple-element.75) | copy-start | bytes 9220
  183.0 34.3 %copy-start.1 = (f32[512,1024]{1,0:T(8,128)S(1)}, f32[512,1024]{1,0:T(8,128)}, u32[]{:S(2)}) copy-start(f32[512,1024]{1,0:T(8,128)} %refs_8_.1) | copy-start | bytes 6291460
  215.4 2.1 copy-start.28
  218.8 109.9 %copy-start.21 = (f32[9,1024]{1,0:T(8,128)S(1)}, f32[9,1024]{1,0:T(8,128)}, u32[]{:S(2)}) copy-start(f32[9,1024]{1,0:T(8,128)} %refs_9_.1) | copy-start | bytes 110596
  218.8 109.9 %copy-start.22 = (f32[9,1024]{1,0:T(8,128)S(1)}, f32[9,1024]{1,0:T(8,128)}, u32[]{:S(2)}) copy-start(f32[9,1024]{1,0:T(8,128)} %param.28) | copy-start | bytes 110596
  218.8 109.9 %copy-start.23 = (f32[9,1024]{1,0:T(8,128)S(1)}, f32[9,1024]{1,0:T(8,128)}, u32[]{:S(2)}) copy-start(f32[9,1024]{1,0:T(8,128)} %param.27) | copy-start | bytes 110596
  218.8 110.7 %copy-start.5 = (f32[1,24,128,128]{3,2,1,0:T(8,128)S(1)}, f32[1,24,128,128]{3,2,1,0:T(8,128)}, u32[]{:S(2)}) copy-start(f32[1,24,128,128]{3,2,1,0:T(8,128)} %param.20) | copy-start | bytes 4718596
  218.8 110.7 %copy-start.6 = (f32[1,24,128,128]{3,2,1,0:T(8,128)S(1)}, f32[1,24,128,128]{3,2,1,0:T(8,128)}, u32[]{:S(2)}) copy-start(f32[1,24,128,128]{3,2,1,0:T(8,128)} %param.21) | copy-start | bytes 4718596
  218.8 110.7 %copy-start.11 = (s32[1,192]{1,0:T(1,128)S(1)}, s32[1,192]{1,0:T(1,128)}, u32[]{:S(2)}) copy-start(s32[1,192]{1,0:T(1,128)} %param.19) | copy-start | bytes 2308
  329.5 2.8 copy-start.3
  332.3 1.4 copy-start.7
  333.7 1.4 copy-start.8
  335.1 1.4 copy-start.9
  336.5 1.4 copy-start.10
  337.9 25.0 %copy-start.24 = (f32[4096]{0:T(1024)S(1)}, f32[4096]{0:T(1024)}, u32[]{:S(2)}) copy-start(f32[4096]{0:T(1024)} %param.29) | copy-start | bytes 49156
  337.9 25.0 %copy-start.25 = (f32[4096]{0:T(1024)S(1)}, f32[4096]{0:T(1024)}, u32[]{:S(2)}) copy-start(f32[4096]{0:T(1024)} %param.31) | copy-start | bytes 49156
  337.9 25.0 %copy-start.26 = (f32[4096]{0:T(1024)S(1)}, f32[4096]{0:T(1024)}, u32[]{:S(2)}) copy-start(f32[4096]{0:T(1024)} %param.30) | copy-start | bytes 49156
  337.9 25.6 %copy-start.20 = (f32[512,1024]{1,0:T(8,128)S(1)}, f32[512,1024]{1,0:T(8,128)}, u32[]{:S(2)}) copy-start(f32[512,1024]{1,0:T(8,128)} %get-tuple-element.118) | copy-start | bytes 6291460
  363.6 2.3 copy-start.19
where the time goes:
time: 371 us; the launch traced here: 367 us
  Pallas kernels  329 us (89%)
  local copies, waits for them, and re-layouts  32.8 us (9%)
  other arithmetic  4.49 us (1%)
    pallas_call x1, Pallas kernels, send_back(): pl.pallas_call(functools.partial(back_kernel, slots, devices), out_shape=...  108 us
    pallas_call x1, Pallas kernels, front(): pl.pallas_call(functools.partial(front_kernel, slots, devices), out_shape...  76.4 us
    pallas_call x2, Pallas kernels, feed_forward(): pl.pallas_call(functools.partial(ff_kernel, len(parts), acc is not None,...  63.4 us
    pallas_call x1, Pallas kernels, attention(): pl.pallas_call(functools.partial(attn_kernel, replicas, replicas), out_sh...  56.6 us
    unnamed x67, local copies, waits for them, and re-layouts  27.5 us
    pallas_call x1, Pallas kernels, soap(): pl.pallas_call(functools.partial(soap_kernel, slots, replicas, per_step),...  24.2 us

commit v1 on v0

v1 whole, which is shorter than its diff:
```python
import functools

import jax
import jax.numpy as jnp
from jax import lax
from jax.experimental import pallas as pl
from jax.experimental.pallas import tpu as pltpu
from jax.sharding import PartitionSpec as P

HEADS = 16
HDIM = 64
ROT = 16
FF = 4096
STEP = 5
TILE = 128
LANES = 128
GROUP = 4

PRECISE = lax.Precision.HIGHEST
eps_norm = 1e-05
eps_adam = 1e-08
lr_matrix = 0.05
lr_vector = 0.5
ema_keep = 0.8

F32 = jnp.float32
BF16 = jnp.bfloat16
ANY = pl.BlockSpec(memory_space=pl.ANY)
VMEM = pl.BlockSpec(memory_space=pltpu.VMEM)
SMEM = pl.BlockSpec(memory_space=pltpu.SMEM)


def dot_nn(left, right):
    return jnp.dot(left, right, preferred_element_type=F32)


def dot_nt(left, right):
    return lax.dot_general(left, right, (((1,), (1,)), ((), ())), preferred_element_type=F32)


def dot_tn(left, right):
    return lax.dot_general(left, right, (((0,), (0,)), ((), ())), preferred_element_type=F32)


def precise(left, right, left_dim, right_dim):
    return lax.dot_general(
        left,
        right,
        (((left_dim,), (right_dim,)), ((), ())),
        precision=PRECISE,
        preferred_element_type=F32,
    )


MESH = pl.DeviceIdType.MESH


def flip(index, mask):
    bit = 1
    while bit <= mask:
        if mask & bit:
            index = index + bit - 2 * bit * ((index // bit) % 2)
        bit *= 2
    return index


def differ(left, right, count):
    total, bit = 0, 1
    while bit < count:
        one, two = (left // bit) % 2, (right // bit) % 2
        total = total + bit * (one + two - 2 * one * two)
        bit *= 2
    return total


class Links:
    def __init__(self, send_sems, recv_sems):
        self.send_sems, self.recv_sems = send_sems, recv_sems
        self.number = 0
        self.all = []

    def send(self, source, target, device):
        copy = pltpu.make_async_remote_copy(
            src_ref=source,
            dst_ref=target,
            send_sem=self.send_sems.at[self.number],
            recv_sem=self.recv_sems.at[self.number],
            device_id=device,
            device_id_type=MESH,
        )
        self.number += 1
        copy.start()
        entry = [copy, False, False]
        self.all.append(entry)
        return entry

    def arrived(self, entry):
        if not entry[1]:
            entry[0].wait_recv()
            entry[1] = True

    def left(self, entry):
        if not entry[2]:
            entry[0].wait_send()
            entry[2] = True

    def finish(self):
        for entry in self.all:
            self.arrived(entry)
            self.left(entry)


def greet(me, column, masks_dp, masks_z):
    barrier = pltpu.get_barrier_semaphore()
    for mask in masks_dp:
        pl.semaphore_signal(barrier, inc=1, device_id={"dp": flip(me, mask)}, device_id_type=MESH)
    for mask in masks_z:
        pl.semaphore_signal(
            barrier, inc=1, device_id={"mlp": flip(column, mask)}, device_id_type=MESH
        )
    pl.semaphore_wait(barrier, len(masks_dp) + len(masks_z))


class Spread:
    def __init__(self, links, slab, me, count, rows, first, size, backward, pairs=True):
        self.links, self.slab, self.me, self.pairs = links, slab, me, pairs
        self.rows, self.first, self.size = rows, first, size
        self.bits = [1 << i for i in range(1, count.bit_length() - 1)]
        if backward:
            self.bits = self.bits[::-1]
        self.came = {}
        self.order = []

    def part(self, at):
        place = at if self.pairs else at // 2
        return self.slab.at[pl.ds(place * self.rows + self.first, self.size)]

    def forward(self, at, step, source=None):
        source = self.part(at) if source is None else source
        for later in range(step, len(self.bits)):
            bit = self.bits[later]
            entry = self.links.send(source, self.part(at ^ bit), {"dp": flip(self.me, bit)})
            self.came[at ^ bit] = (entry, later + 1)
            self.order.append(at ^ bit)
        if self.pairs:
            self.links.send(source, self.part(at ^ 1), {"dp": flip(self.me, 1)})

    def relay(self):
        while self.order:
            at = min(self.order, key=lambda index: (self.came[index][1], index.bit_count()))
            self.order.remove(at)
            entry, step = self.came[at]
            self.links.arrived(entry)
            self.forward(at, step)


def attn_unit(column, rank, place):
    by_columns = (place // 2) * 8 + 2 * rank + place % 2
    by_rows = (2 * rank + place // 8) * 8 + place % 8
    return jnp.where(column == 3, by_rows, by_columns)


def ff_unit(core, place):
    later = place - 32
    up = 64 + (place // 4) * 8 + core * 4 + place % 4
    down = 128 + (core * 4 + later // 8) * 8 + later % 8
    return jnp.where(place < 32, up, down)


def front_kernel(slots, devices, tokens, cot, table, masters, tile_ref, *refs):
    (hats, cots, tables, attn_parts, own_attn, own_ff, send_ff) = refs[:7]
    (slab, own_hat, own_cot, send_attn, send_sems, recv_sems, local_sems) = refs[7:]
    me, column = lax.axis_index("dp"), lax.axis_index("mlp")
    replicas = devices // 2
    core, quarter, low = me % 2, me // 2, column % 2
    links = Links(send_sems, recv_sems)
    half = slots // 2
    greet(me, column, [1] + [at << 1 for at in range(1, replicas)], [1, 2, 3])
    slab[0:slots] = masters[...].astype(BF16)
    spreads = [
        Spread(links, slab, me, devices, slots, 0, half, False),
        Spread(links, slab, me, devices, slots, half, slots - half, True),
    ]
    for spread in spreads:
        spread.forward(0, 0)

    length = tokens.shape[0]
    step_rows = 128

    def normalize(step, carry):
        where = pl.ds(pl.multiple_of(step * step_rows, step_rows), step_rows)
        value = tokens[where, :]
        value = value - jnp.mean(value, axis=-1, keepdims=True)
        value = value * lax.rsqrt(jnp.mean(value * value, axis=-1, keepdims=True) + eps_norm)
        own_hat[where, :] = value.astype(BF16)
        own_cot[where, :] = cot[where, :].astype(BF16)
        return carry

    lax.fori_loop(0, length // step_rows, normalize, 0)
    own = []
    along = []

    def send_along(source, target, where):
        entry = links.send(source.at[where], target.at[2].at[where], {"mlp": flip(column, 1)})
        along.append((target, where, entry))

    for number, (source, target) in enumerate(
        ((own_hat, hats), (table, tables), (own_cot, cots))
    ):
        send_along(source, target, pl.ds(0, source.shape[0] // (2 if number == 2 else 1)))
        links.send(source, target.at[1], {"dp": flip(me, 1)})
        copy = pltpu.make_async_copy(source, target.at[0], local_sems.at[number])
        copy.start()
        own.append(copy)
    for spread in spreads:
        spread.relay()
    for entry in links.all:
        if not any(entry is item[2] for item in along):
            links.arrived(entry)

    def fill(out_ref, base, rows_out, first_row, unit_of):
        size = min(TILE, rows_out)

        def body(step, carry):
            row = first_row + step * size
            tile = tile_ref[unit_of(row // TILE)]
            where = pl.ds(pl.multiple_of(base + step * size, size), size)
            if size == TILE:
                out_ref[where, :] = slab[tile]
            else:
                out_ref[where, :] = slab[tile, pl.ds(pl.multiple_of(row % TILE, size), size), :]
            return carry

        lax.fori_loop(0, rows_out // size, body, 0)

    rows_attn = 16 * TILE // replicas
    across = []
    for bit in (3, 2, 1):
        rank = 2 * (flip(low, 1) if bit & 1 else low) + core
        base = (bit - 1) * rows_attn
        fill(
            send_attn,
            base,
            rows_attn,
            quarter * rows_attn,
            functools.partial(attn_unit, column, rank),
        )
        piece = pl.ds(base, rows_attn)
        across.append(
            (
                piece,
                links.send(
                    send_attn.at[piece, :],
                    attn_parts.at[piece, :],
                    {"mlp": flip(column, bit)},
                ),
            )
        )
    send_along(own_cot, cots, pl.ds(length // 2, length // 2))
    rows_ff = 64 * TILE // replicas
    fill(own_attn, 0, 16 * TILE, 0, functools.partial(attn_unit, column, 2 * low + core))
    spreads = []
    for number, (piece, entry) in enumerate(across[::-1]):
        links.arrived(entry)
        pieces = [(number * rows_attn, rows_attn, number == 1)]
        if number == 2:
            cut = rows_attn // 32 * 16
            pieces = [
                (2 * rows_attn, cut, False),
                (2 * rows_attn + cut, rows_attn - cut, True),
            ]
        for first, size, backward in pieces:
            spreads.append(
                Spread(links, attn_parts, me, devices, 3 * rows_attn, first, size, backward, False)
            )
            spreads[-1].forward(0, 0)
    fill(send_ff, 0, rows_ff, quarter * rows_ff, functools.partial(ff_unit, core))
    fill(own_ff, 0, 64 * TILE, 0, functools.partial(ff_unit, core))
    for spread in spreads:
        spread.relay()
    for target, where, entry in along:
        links.arrived(entry)
        links.send(target.at[2].at[where], target.at[3].at[where], {"dp": flip(me, 1)})
    for copy in own:
        copy.wait()
    links.finish()


def front(tokens, cot, table, masters, tile_row):
    length, width = tokens.shape
    slots = masters.shape[0]
    devices = lax.axis_size("dp")
    replicas = devices // 2
    rows_attn = 16 * TILE // replicas
    count = 2 * (2 * replicas - 1) + 11 + 3 + 4 * (replicas - 1)
    block = jax.ShapeDtypeStruct((4, length, width), BF16)
    flat = lambda number: jax.ShapeDtypeStruct((number, LANES), BF16)
    return pl.pallas_call(
        functools.partial(front_kernel, slots, devices),
        out_shape=[
            block,
            block,
            jax.ShapeDtypeStruct((4,) + table.shape, F32),
            jax.ShapeDtypeStruct((replicas * 3 * rows_attn, LANES), BF16),
            flat(16 * TILE),
            flat(64 * TILE),
            flat(64 * TILE // replicas),
        ],
        in_specs=[VMEM] * 4 + [SMEM],
        out_specs=[ANY] * 4 + [VMEM] * 3,
        scratch_shapes=[
            pltpu.VMEM((devices * slots, TILE, LANES), BF16),
            pltpu.VMEM((length, width), BF16),
            pltpu.VMEM((length, width), BF16),
            pltpu.VMEM((3 * rows_attn, LANES), BF16),
            pltpu.SemaphoreType.DMA((count,)),
            pltpu.SemaphoreType.DMA((count,)),
            pltpu.SemaphoreType.DMA((3,)),
        ],
        compiler_params=pltpu.CompilerParams(
            vmem_limit_bytes=60 << 20, collective_id=0, has_side_effects=True
        ),
        cost_estimate=pl.CostEstimate(flops=0, bytes_accessed=200 << 20, transcendentals=0),
        name="front",
    )(tokens, cot, table, masters, tile_row)


def erf_f32(value):
    value = jnp.clip(value, -3.832506856900711, 3.832506856900711)
    square = value * value
    top = jnp.full_like(square, 0.00022905065861350646)
    for coeff in (
        0.0034082910107109506,
        0.050955695062380861,
        0.18520832239976145,
        1.128379143519084,
    ):
        top = top * square + coeff
    low = jnp.full_like(square, -1.1791602954361697e-7)
    for coeff in (
        0.000023547966471313185,
        0.0010179625278914885,
        0.014070470171167667,
        0.11098505178285362,
        0.49746925110067538,
        1.0,
    ):
        low = low * square + coeff
    return value * top / low


def row_sum(value):
    return dot_nn(jnp.ones((16, value.shape[0]), BF16), value)[0:1, :]


def transpose_tile(value):
    return jnp.swapaxes(value, 0, 1)


def middle_kernel(slots, devices, *refs):
    refs = list(refs)
    take = lambda number: [refs.pop(0) for _ in range(number)]
    norm_ref, hidden_ref, table_ref, hats, cots = take(5)
    own_attn, attn_parts, own_ff, send_ff = take(4)
    mine, across, slab, reduced = take(4)
    h_all, c_all, out_acc, back_acc = take(4)
    tiles, up, down, up_acc, down_acc = take(5)
    w_in, w_out, in_acc, proj_acc = take(4)
    q_all, k_all, v_all, g_all, o_all, dq_all, dk_all, dv_all = take(8)
    dw, own_land, attn_land, z_ff, core_land = take(5)
    own_sum, attn_keep, attn_send, attn_back, z_send, z_land, block_all = take(7)
    vec, vec_land, vec_sum = take(3)
    local_sems, tile_sems, send_sems, recv_sems = take(4)
    me, column = lax.axis_index("dp"), lax.axis_index("mlp")
    replicas = devices // 2
    core, quarter = me % 2, me // 2
    rank = 2 * (column % 2) + core
    length, width = h_all.shape[1:]
    hidden = up.shape[1]
    wide = 4 * HDIM
    rows_ff, rows_attn = 64 * TILE // replicas, 16 * TILE // replicas
    loads = []
    tile_load = pltpu.make_async_copy(own_ff, tiles, local_sems.at[8])
    tile_load.start()
    for number in range(4):
        pair = []
        for source, target, sem in ((hats, h_all, number), (cots, c_all, 4 + number)):
            copy = pltpu.make_async_copy(source.at[number], target.at[number], local_sems.at[sem])
            copy.start()
            pair.append(copy)
        loads.append(pair)
    links = Links(send_sems, recv_sems)
    greet(me, column, [1] + [at << 1 for at in range(1, replicas)], [1, 2, 3])
    came_ff = [links.send(send_ff, z_ff.at[0], {"mlp": flip(column, 2)})]
    vec[...] = jnp.zeros_like(vec)

    def set_ff_weights():
        for at in range(32):
            up[
                (at // 4) * TILE : (at // 4 + 1) * TILE, (at % 4) * TILE : (at % 4 + 1) * TILE
            ] = tiles[at * TILE : (at + 1) * TILE, :]
            down[
                (at // 8) * TILE : (at // 8 + 1) * TILE, (at % 8) * TILE : (at % 8 + 1) * TILE
            ] = tiles[(32 + at) * TILE : (33 + at) * TILE, :]
        up_acc[...] = jnp.zeros_like(up_acc)
        down_acc[...] = jnp.zeros_like(down_acc)

    def ff_block(at, ff_column, first, store):
        hat = h_all[at].astype(F32)
        normed = (hat * norm_ref[2:3, :] + norm_ref[3:4, :]).astype(BF16)
        cot = c_all[at]
        pre = dot_nn(normed, up[...]) + hidden_ref[pl.ds(2 * ff_column + core, 1), :]
        cdf = 0.5 + 0.5 * erf_f32(pre * 0.7071067811865476)
        act = (pre * cdf).astype(BF16)
        grad = dot_nt(cot, down[...])
        grad = grad * (cdf + pre * (jnp.exp(-0.5 * pre * pre) * 0.3989422804014327))
        grad = grad.astype(BF16)
        where = pl.ds(pl.multiple_of(core * hidden, hidden), hidden)
        vec[pl.ds(8 + ff_column, 1), where] += row_sum(grad)
        out = dot_nn(act, down[...])
        back = dot_nt(grad, up[...])
        vec[2:3, :] += jnp.sum(back * hat, axis=0, keepdims=True)
        vec[3:4, :] += jnp.sum(back, axis=0, keepdims=True)
        back = back * norm_ref[2:3, :]
        if not first:
            out = out + out_acc[at].astype(F32)
            back = back + back_acc[at].astype(F32)
        store(out, back)
        up_acc[...] += dot_tn(normed, grad)
        down_acc[...] += dot_tn(act, cot)

    def store_ff(target):
        per = rows_ff // TILE
        for at in range(64):
            if at < 32:
                tile = up_acc[
                    (at // 4) * TILE : (at // 4 + 1) * TILE, (at % 4) * TILE : (at % 4 + 1) * TILE
                ]
            else:
                low = at - 32
                tile = down_acc[
                    (low // 8) * TILE : (low // 8 + 1) * TILE,
                    (low % 8) * TILE : (low % 8 + 1) * TILE,
                ]
            target[
                differ(at // per, quarter, replicas), (at % per) * TILE : (at % per + 1) * TILE, :
            ] = tile.astype(BF16)

    def attn_rows(matrix):
        return pl.multiple_of(matrix * (16 * TILE), TILE)

    tile_load.wait()
    set_ff_weights()
    tile_loads = [
        pltpu.make_async_copy(
            own_attn, tiles.at[pl.ds(attn_rows(column), 16 * TILE), :], tile_sems.at[0]
        )
    ]
    for at in range(replicas):
        for bit in (1, 2, 3):
            first = attn_rows(flip(column, bit)) + differ(at, quarter, replicas) * rows_attn
            tile_loads.append(
                pltpu.make_async_copy(
                    attn_parts.at[pl.ds((3 * at + bit - 1) * rows_attn, rows_attn), :],
                    tiles.at[pl.ds(pl.multiple_of(first, rows_attn), rows_attn), :],
                    tile_sems.at[len(tile_loads)],
                )
            )
    for copy in tile_loads:
        copy.start()
    for at in range(4):
        for copy in loads[at]:
            copy.wait()
    vec[7:8, :] = row_sum(c_all[0])

    def own_block(at, carry):
        def store(out, back):
            out_acc[at] = out.astype(BF16)
            back_acc[at] = back.astype(BF16)

        ff_block(at, column, True, store)
        return carry

    lax.fori_loop(0, 4, own_block, 0)
    store_ff(dw)
    own_sum[...] = dw[0].astype(F32)
    own_came = [
        links.send(dw.at[at], own_land.at[at - 1], {"dp": flip(me, at << 1)})
        for at in range(1, replicas)
    ]
    links.arrived(came_ff[0])
    for at in range(1, replicas):
        came_ff.append(links.send(z_ff.at[0], z_ff.at[at], {"dp": flip(me, at << 1)}))

    for copy in tile_loads:
        copy.wait()
    for matrix in range(3):
        for at in range(16):
            row = (16 * matrix + at) * TILE
            w_in[
                (at // 2) * TILE : (at // 2 + 1) * TILE,
                (2 * matrix + at % 2) * TILE : (2 * matrix + at % 2 + 1) * TILE,
            ] = tiles[row : row + TILE, :]
    for at in range(16):
        w_out[(at // 8) * TILE : (at // 8 + 1) * TILE, (at % 8) * TILE : (at % 8 + 1) * TILE] = (
            tiles[(48 + at) * TILE : (49 + at) * TILE, :]
        )
    in_acc[...] = jnp.zeros_like(in_acc)
    proj_acc[...] = jnp.zeros_like(proj_acc)
    half = ROT // 2
    block = BLOCK
    scale = HDIM ** (-0.5)
    lane = lax.broadcasted_iota(jnp.int32, (1, LANES), 1)
    within = lane % HDIM
    keep_low = lane < HDIM
    wave = lax.broadcasted_iota(jnp.int32, (ROT, LANES), 0)
    spot = lax.broadcasted_iota(jnp.int32, (ROT, LANES), 1) % HDIM
    pick_cos = ((spot < ROT) & (wave == spot % half)).astype(F32)
    pick_first = ((spot < half) & (wave == half + spot)).astype(F32)
    pick_second = ((spot >= half) & (spot < ROT) & (wave == spot)).astype(F32)
    plain = (within >= ROT).astype(F32)

    def attn_block(at, carry):
        hat = h_all[at].astype(F32)
        normed = (hat * norm_ref[0:1, :] + norm_ref[1:2, :]).astype(BF16)
        cot = c_all[at]
        table = table_ref[at]
        cos_w = precise(table, pick_cos, 0, 0) + plain
        sin_a = precise(table, pick_first, 0, 0)
        sin_b = precise(table, pick_second, 0, 0)
        proj = dot_nn(normed, w_in[...])
        g_all[...] = dot_nt(cot, w_out[...]).astype(BF16)

        def turn(value):
            return (
                value * cos_w
                - pltpu.roll(value, LANES - half, 1) * sin_a
                + pltpu.roll(value, half, 1) * sin_b
            )

        for pair in range(2):
            cols = slice(pair * LANES, (pair + 1) * LANES)
            where = pl.ds(pl.multiple_of(rank * wide + pair * LANES, LANES), LANES)
            query = proj[:, pair * LANES : (pair + 1) * LANES] + norm_ref[4:5, where]
            key = proj[:, wide + pair * LANES : wide + (pair + 1) * LANES] + norm_ref[5:6, where]
            value = proj[:, 2 * wide + pair * LANES : 2 * wide + (pair + 1) * LANES]
            q_all[:, cols] = (turn(query).astype(BF16) * scale).astype(BF16)
            k_all[:, cols] = turn(key).astype(BF16)
            v_all[:, cols] = (value + norm_ref[6:7, where]).astype(BF16)
        zero = jnp.zeros((), BF16)
        for pair in range(2):
            cols = slice(pair * LANES, (pair + 1) * LANES)
            query, key = q_all[:, cols], k_all[:, cols]
            value, grad = v_all[:, cols], g_all[:, cols]
            key_t, value_t = transpose_tile(key), transpose_tile(value)
            out_t, dq_t = [], []
            dk_all[:, cols] = jnp.zeros((length, LANES), F32)
            dv_all[:, cols] = jnp.zeros((length, LANES), F32)
            for head in range(2):
                mask = keep_low if head == 0 else jnp.logical_not(keep_low)
                key_m, value_m = jnp.where(mask, key, zero), jnp.where(mask, value, zero)
                query_m, grad_m = jnp.where(mask, query, zero), jnp.where(mask, grad, zero)
                part = slice(head * HDIM, (head + 1) * HDIM)
                out_row, dq_row = [], []
                for first in range(0, length, block):
                    last = first + block
                    scores = dot_nt(key_m[:last], query[first:last])
                    key_at = lax.broadcasted_iota(jnp.int32, scores.shape, 0)
                    query_at = first + lax.broadcasted_iota(jnp.int32, scores.shape, 1)
                    scores = jnp.where(key_at <= query_at, scores, -1e30)
                    peak = jnp.max(scores, axis=0, keepdims=True)
                    raised = jnp.exp(scores - peak)
                    prob = raised * (1.0 / jnp.sum(raised, axis=0, keepdims=True))
                    prob_low = prob.astype(BF16)
                    grad_prob = dot_nt(value_m[:last], grad[first:last])
                    delta = jnp.sum(prob * grad_prob, axis=0, keepdims=True)
                    grad_scores = (prob * (grad_prob - delta)).astype(BF16)
                    out_row.append(dot_nn(value_t[part, :last], prob_low))
                    dq_row.append(dot_nn(key_t[part, :last], grad_scores))
                    dv_all[:last, cols] += dot_nn(prob_low, grad_m[first:last])
                    dk_all[:last, cols] += dot_nn(grad_scores, query_m[first:last])
                out_t.append(jnp.concatenate(out_row, axis=1))
                dq_t.append(jnp.concatenate(dq_row, axis=1))
            o_all[:, cols] = transpose_tile(jnp.concatenate(out_t, axis=0)).astype(BF16)
            dq_all[:, cols] = transpose_tile(jnp.concatenate(dq_t, axis=0)) * scale

        def turn_back(value):
            return (
                value * cos_w
                + pltpu.roll(value, LANES - half, 1) * sin_a
                - pltpu.roll(value, half, 1) * sin_b
            ).astype(BF16)

        pieces = [turn_back(dq_all[:, 0:LANES]), turn_back(dq_all[:, LANES : 2 * LANES])]
        pieces += [turn_back(dk_all[:, 0:LANES]), turn_back(dk_all[:, LANES : 2 * LANES])]
        pieces += [dv_all[...].astype(BF16)]
        grads = jnp.concatenate(pieces, axis=1)
        sums = row_sum(grads)
        where = pl.ds(pl.multiple_of(rank * wide, LANES), wide)
        for matrix in range(3):
            vec[4 + matrix : 5 + matrix, where] += sums[:, matrix * wide : (matrix + 1) * wide]
        out = dot_nn(o_all[...], w_out[...])
        out_acc[at] = (out_acc[at].astype(F32) + out).astype(BF16)
        back = dot_nt(grads, w_in[...])
        vec[0:1, :] += jnp.sum(back * hat, axis=0, keepdims=True)
        vec[1:2, :] += jnp.sum(back, axis=0, keepdims=True)
        back_acc[at] = (back_acc[at].astype(F32) + back * norm_ref[0:1, :]).astype(BF16)
        in_acc[...] += dot_tn(normed, grads)
        proj_acc[...] += dot_tn(o_all[...], cot)
        return carry

    lax.fori_loop(0, 4, attn_block, 0)
    for entry in own_came:
        links.arrived(entry)
        links.left(entry)
    for at in range(1, replicas):
        own_sum[...] += own_land[at - 1].astype(F32)
    size = min(TILE, rows_attn)
    for matrix in range(4):
        for at in range(16):
            for piece in range(TILE // size):
                row = at * TILE + piece * size
                if matrix < 3:
                    top, left = (at // 2) * TILE, (2 * matrix + at % 2) * TILE
                    tile = in_acc[top + piece * size : top + (piece + 1) * size, left : left + TILE]
                else:
                    top, left = (at // 8) * TILE, (at % 8) * TILE
                    tile = proj_acc[
                        top + piece * size : top + (piece + 1) * size, left : left + TILE
                    ]
                inner = row % rows_attn
                dw[
                    differ(row // rows_attn, quarter, replicas),
                    pl.ds(
                        pl.multiple_of(flip(column, matrix) * rows_attn + inner, size), size
                    ),
                    :,
                ] = tile.astype(BF16)
    attn_came = [
        links.send(dw.at[at], attn_land.at[at - 1], {"dp": flip(me, at << 1)})
        for at in range(1, replicas)
    ]
    attn_keep[...] = dw[0, 0:rows_attn, :].astype(F32)
    attn_send[...] = dw[0, rows_attn : 4 * rows_attn, :]

    other = flip(column, 2)
    for entry in came_ff:
        links.arrived(entry)
    for at in range(replicas):
        first = differ(at, quarter, replicas) * rows_ff
        tiles[pl.ds(pl.multiple_of(first, TILE), rows_ff), :] = z_ff[at]
    set_ff_weights()
    core_came = {}
    outs = []
    waiting = []

    def pump(count):
        for number, source, where in waiting[:count]:
            links.send(
                source.at[2, where, :], across.at[number, where, :], {"mlp": flip(column, 1)}
            )
        del waiting[:count]

    def send_core(at):
        def store(out, back):
            out_acc[at] = out.astype(BF16)
            back_acc[at] = back.astype(BF16)
            for number, source in ((0, out_acc), (1, back_acc)):
                core_came[number, at // 2] = links.send(
                    source.at[at], core_land.at[number, at // 2], {"dp": flip(me, 1)}
                )

        return store

    def keep(at):
        def store(out, back):
            for number, value, source in ((0, out, out_acc), (1, back, back_acc)):
                links.arrived(core_came[number, at // 2])
                value = value + core_land[number, at // 2].astype(F32)
                source[at] = value.astype(BF16)
                if at == 0:
                    copy = pltpu.make_async_copy(
                        source.at[at], mine.at[number], local_sems.at[number]
                    )
                    copy.start()
                    outs.append(copy)
                else:
                    for first in range(0, length, length // 4):
                        waiting.append((number, source, pl.ds(first, length // 4)))

        return store

    for at in (3, 2, 1, 0):
        ff_block(at, other, False, send_core(at) if at % 2 else keep(at))
        pump(1)
    for entry in attn_came:
        links.arrived(entry)
        links.left(entry)

    store_ff(dw)
    chunks = 4
    size = rows_ff // chunks
    dw_came = []
    for chunk in range(chunks):
        piece = pl.ds(chunk * size, size)
        dw_came.append(
            [
                links.send(
                    dw.at[at, piece, :], own_land.at[at - 1, piece, :], {"dp": flip(me, at << 1)}
                )
                for at in range(1, replicas)
            ]
        )
    vec_came = [
        links.send(vec, vec_land.at[bit], {"mlp": flip(column, bit)}) for bit in (1, 2, 3)
    ]
    for at in range(1, replicas):
        attn_keep[...] += attn_land[at - 1, 0:rows_attn, :].astype(F32)
    total = attn_send[...].astype(F32)
    for at in range(1, replicas):
        total = total + attn_land[at - 1, rows_attn : 4 * rows_attn, :].astype(F32)
    attn_send[...] = total.astype(BF16)
    back_came = []
    for bit in (1, 2, 3):
        piece = pl.ds((bit - 1) * rows_attn, rows_attn)
        back_came.append(
            links.send(attn_send.at[piece, :], attn_back.at[bit - 1], {"mlp": flip(column, bit)})
        )
    pump(1)
    rows = slots * TILE
    spreads = []

    def publish(first, count):
        backward = len(spreads) % 2 == 1
        spread = Spread(links, slab, me, devices, rows, first, count, backward)
        source = block_all.at[pl.ds(first, count), :]
        spread.forward(0, 0, source)
        copy = pltpu.make_async_copy(source, spread.part(0), local_sems.at[2 + len(spreads)])
        copy.start()
        outs.append(copy)
        spreads.append(spread)

    def add_chunk(chunk):
        piece = slice(chunk * size, (chunk + 1) * size)
        for entry in dw_came[chunk]:
            links.arrived(entry)
        total = dw[0, piece, :].astype(F32)
        for at in range(1, replicas):
            total = total + own_land[at - 1, piece, :].astype(F32)
        z_send[piece, :] = total.astype(BF16)
        where = pl.ds(chunk * size, size)
        return links.send(z_send.at[where, :], z_land.at[where, :], {"mlp": flip(column, 2)})

    for entry in vec_came:
        links.arrived(entry)
    vec_sum[0] = (vec[...] + vec_land[1]) + (vec_land[2] + vec_land[3])
    vec_core = links.send(vec_sum.at[0], vec_land.at[0], {"dp": flip(me, 1)})
    z_came = [add_chunk(0)]
    pump(1)
    for entry in back_came:
        links.arrived(entry)
    block_all[rows_ff : rows_ff + rows_attn, :] = (
        attn_keep[...] + attn_back[1].astype(F32)
    ).astype(BF16)
    publish(rows_ff, rows_attn)
    block_all[rows_ff + rows_attn : rows, :] = (
        attn_back[0].astype(F32) + attn_back[2].astype(F32)
    ).astype(BF16)
    publish(rows_ff + rows_attn, rows_attn)
    links.arrived(vec_core)
    vec_sum[1] = vec_sum[0] + vec_land[0]
    vec_came = [
        links.send(vec_sum.at[1], vec_land.at[3 + at], {"dp": flip(me, at << 1)})
        for at in range(1, replicas)
    ]
    for chunk in range(1, chunks):
        z_came.append(add_chunk(chunk))
        pump(1)
    for spread in spreads[:2]:
        spread.relay()
    for chunk in range(chunks):
        links.arrived(z_came[chunk])
        piece = slice(chunk * size, (chunk + 1) * size)
        block_all[piece, :] = (own_sum[piece, :] + z_land[piece, :].astype(F32)).astype(BF16)
        publish(chunk * size, size)
        pump(1)
        if chunk > 0:
            spreads[1 + chunk].relay()
    pump(len(waiting))
    spreads[1 + chunks].relay()
    for entry in vec_came:
        links.arrived(entry)
    values = [vec_sum[1]] + [vec_land[3 + at] for at in range(1, replicas)]
    while len(values) > 1:
        values = [values[i] + values[i + 1] for i in range(0, len(values), 2)]
    reduced[...] = values[0]
    for copy in outs:
        copy.wait()
    links.finish()


BLOCK = 256


def middle(vectors, hidden_bias, tables, hats, cots, own_attn, attn_parts, own_ff, send_ff, slots):
    length, width = hats.shape[1:]
    devices = lax.axis_size("dp")
    replicas = devices // 2
    hidden = 4 * TILE
    wide = 4 * HDIM
    rows_ff, rows_attn = 64 * TILE // replicas, 16 * TILE // replicas
    count = 1 + 3 * (replicas - 1) + 4 + 8 + 4 * (replicas - 1) + 3 + 3 + 4 + 1 + replicas - 1
    count += 6 * (2 * replicas - 1)
    rows = slots * TILE
    vmem = lambda *shape: pltpu.VMEM(shape, BF16)
    vmem32 = lambda *shape: pltpu.VMEM(shape, F32)
    return pl.pallas_call(
        functools.partial(middle_kernel, slots, devices),
        out_shape=[
            jax.ShapeDtypeStruct((2, length, width), BF16),
            jax.ShapeDtypeStruct((2, length, width), BF16),
            jax.ShapeDtypeStruct((devices * rows, LANES), BF16),
            jax.ShapeDtypeStruct((12, width), F32),
        ],
        in_specs=[VMEM] * 3 + [ANY] * 6,
        out_specs=[ANY] * 3 + [VMEM],
        scratch_shapes=[
            vmem(4, length, width),
            vmem(4, length, width),
            vmem(4, length, width),
            vmem(4, length, width),
            vmem(64 * TILE, LANES),
            vmem(width, hidden),
            vmem(hidden, width),
            vmem32(width, hidden),
            vmem32(hidden, width),
            vmem(width, 3 * wide),
            vmem(wide, width),
            vmem32(width, 3 * wide),
            vmem32(wide, width),
            vmem(length, wide),
            vmem(length, wide),
            vmem(length, wide),
            vmem(length, wide),
            vmem(length, wide),
            vmem32(length, wide),
            vmem32(length, wide),
            vmem32(length, wide),
            vmem(replicas, rows_ff, LANES),
            vmem(replicas - 1, rows_ff, LANES),
            vmem(replicas - 1, 4 * rows_attn, LANES),
            vmem(replicas, rows_ff, LANES),
            vmem(2, 2, length, width),
            vmem32(rows_ff, LANES),
            vmem32(rows_attn, LANES),
            vmem(3 * rows_attn, LANES),
            vmem(3, rows_attn, LANES),
            vmem(rows_ff, LANES),
            vmem(rows_ff, LANES),
            vmem(rows, LANES),
            vmem32(12, width),
            vmem32(3 + replicas, 12, width),
            vmem32(2, 12, width),
            pltpu.SemaphoreType.DMA((9,)),
            pltpu.SemaphoreType.DMA((3 * replicas + 1,)),
            pltpu.SemaphoreType.DMA((count,)),
            pltpu.SemaphoreType.DMA((count,)),
        ],
        compiler_params=pltpu.CompilerParams(
            vmem_limit_bytes=63 << 20, collective_id=2, has_side_effects=True
        ),
        cost_estimate=pl.CostEstimate(
            flops=60 * 10**9, bytes_accessed=40 << 20, transcendentals=0
        ),
        name="middle",
    )(vectors, hidden_bias, tables, hats, cots, own_attn, attn_parts, own_ff, send_ff)


def split(value):
    high = value.astype(BF16)
    return high, (value - high.astype(F32)).astype(BF16)


def soap_kernel(slots, replicas, per_step, *refs):
    refs = list(refs)
    take = lambda number: [refs.pop(0) for _ in range(number)]
    place_ref, owner_ref, slab = take(3)
    left_ref, right_ref, first_ref, second_ref, master_ref, ema_ref = take(6)
    grad_ref, first_out, second_out, master_out, copy_out, ema_out = take(6)
    mine, inverse, sem = take(3)
    me, column = place_ref[0], place_ref[1]
    step = pl.program_id(0)
    bias_fix = 1.0 - 0.5**STEP
    rows_ff = 64 * TILE // replicas
    rows_attn = 16 * TILE // replicas
    rows_all = slots * TILE
    size = min(TILE, rows_attn)

    @pl.when(step == 0)
    def _():
        def note(unit, carry):
            inverse[owner_ref[unit]] = unit
            return carry

        lax.fori_loop(0, owner_ref.shape[0], note, 0)

        def fetch(number, carry):
            unit = inverse[me * slots + number]
            row, col = (unit % 64) // 8, unit % 8
            by_rows = column == 3
            rank = jnp.where(by_rows, row // 2, col // 2)
            attn_place = jnp.where(by_rows, (row % 2) * 8 + col, row * 2 + col % 2)
            up_place = row * 4 + col % 4
            down_place = 32 + (row % 4) * 8 + col
            is_attn, is_up = unit < 64, unit < 128
            core = jnp.where(is_attn, rank % 2, jnp.where(is_up, col // 4, row // 4))
            other = ((rank // 2) != (column % 2)).astype(jnp.int32)
            for piece in range(TILE // size):
                attn_row = attn_place * TILE + piece * size
                ff_row = jnp.where(is_up, up_place, down_place) * TILE + piece * size
                holder = jnp.where(is_attn, attn_row // rows_attn, ff_row // rows_ff)
                inner = jnp.where(
                    is_attn, rows_ff + other * rows_attn + attn_row % rows_attn, ff_row % rows_ff
                )
                start = ((holder * 2 + core) ^ me) * rows_all + inner
                pltpu.make_async_copy(
                    slab.at[pl.ds(pl.multiple_of(start, size), size), :],
                    mine.at[number, pl.ds(piece * size, size), :],
                    sem,
                ).start()
            return carry

        lax.fori_loop(0, slots, fetch, 0)
        pltpu.make_async_copy(mine, mine, sem).wait()

    every = range(per_step)
    grads = [mine[step * per_step + number] for number in every]
    left = [split(left_ref[number]) for number in every]
    right = [split(right_ref[number]) for number in every]
    twice = lambda value, axis: jnp.concatenate([value, value], axis=axis)
    both = lambda pair, axis: jnp.concatenate(pair, axis=axis)
    turned = [dot_tn(both(left[n], 0), twice(grads[n], 0)) for n in every]
    parts = [split(turned[n]) for n in every]
    turned = [
        dot_nn(parts[n][0], right[n][1]) + dot_nn(both(parts[n], 1), twice(right[n][0], 0))
        for n in every
    ]
    scaled = []
    for n in every:
        grad_ref[n] = grads[n].astype(F32)
        first = 0.5 * first_ref[n] + 0.5 * turned[n]
        second = 0.5 * second_ref[n] + 0.5 * turned[n] * turned[n]
        first_out[n] = first
        second_out[n] = second
        scaled.append(first / bias_fix / (jnp.sqrt(second / bias_fix) + eps_adam))
    parts = [split(scaled[n]) for n in every]
    back = [
        dot_nn(left[n][0], parts[n][1]) + dot_nn(both(left[n], 1), twice(parts[n][0], 0))
        for n in every
    ]
    parts = [split(back[n]) for n in every]
    back = [
        dot_nt(parts[n][0], right[n][1]) + dot_nt(both(parts[n], 1), twice(right[n][0], 1))
        for n in every
    ]
    for n in every:
        master = master_ref[n] - lr_matrix * back[n]
        master_out[n] = master
        copy_out[n] = master.astype(BF16)
        ema_out[n] = ema_keep * ema_ref[n] + (1.0 - ema_keep) * master


def soap(place, owner_row, slab, state, replicas):
    slots = state[0].shape[0]
    per_step = 4 if slots % 4 == 0 else 1
    spec = pl.BlockSpec((per_step, TILE, TILE), lambda i: (i, 0, 0))
    shape = (slots, TILE, TILE)
    return pl.pallas_call(
        functools.partial(soap_kernel, slots, replicas, per_step),
        grid=(slots // per_step,),
        out_shape=[jax.ShapeDtypeStruct(shape, F32)] * 4
        + [jax.ShapeDtypeStruct(shape, BF16), jax.ShapeDtypeStruct(shape, F32)],
        in_specs=[SMEM, SMEM, ANY] + [spec] * 6,
        out_specs=[spec] * 6,
        scratch_shapes=[
            pltpu.VMEM(shape, BF16),
            pltpu.SMEM((owner_row.shape[0],), jnp.int32),
            pltpu.SemaphoreType.DMA,
        ],
        compiler_params=pltpu.CompilerParams(vmem_limit_bytes=60 << 20),
        cost_estimate=pl.CostEstimate(
            flops=24 * slots * 2 * TILE**3, bytes_accessed=20 << 20, transcendentals=0
        ),
        name="soap",
    )(place, owner_row, slab, *state)


def finish_kernel(tokens, cot, mine, across, bias, result, grad_tokens):
    value = tokens[...]
    out = mine[0].astype(F32) + across[0].astype(F32)
    result[...] = value + (out + (bias[7:8, :] + bias[8:9, :]))
    value = value - jnp.mean(value, axis=-1, keepdims=True)
    inverse = lax.rsqrt(jnp.mean(value * value, axis=-1, keepdims=True) + eps_norm)
    hat = value * inverse
    grad = mine[1].astype(F32) + across[1].astype(F32)
    grad_tokens[...] = cot[...] + inverse * (
        grad
        - jnp.mean(grad, axis=-1, keepdims=True)
        - hat * jnp.mean(grad * hat, axis=-1, keepdims=True)
    )


def finish(tokens, cot, mine, across, vectors):
    length, width = tokens.shape
    rows = 128
    one = pl.BlockSpec((rows, width), lambda i: (i, 0))
    two = pl.BlockSpec((2, rows, width), lambda i: (0, i, 0))
    whole = pl.BlockSpec(vectors.shape, lambda i: (0, 0))
    return pl.pallas_call(
        finish_kernel,
        grid=(length // rows,),
        out_shape=[jax.ShapeDtypeStruct((length, width), F32)] * 2,
        in_specs=[one, one, two, two, whole],
        out_specs=[one, one],
        compiler_params=pltpu.CompilerParams(vmem_limit_bytes=60 << 20),
        cost_estimate=pl.CostEstimate(flops=0, bytes_accessed=12 << 20, transcendentals=0),
        name="finish",
    )(tokens, cot, mine, across, vectors)


def adam_step(grad, first, second, param):
    bias_fix = 1.0 - 0.5**STEP
    first_new = 0.5 * first + 0.5 * grad
    second_new = 0.5 * second + 0.5 * grad * grad
    return (
        first_new,
        second_new,
        param - lr_vector * (first_new / bias_fix) / (jnp.sqrt(second_new / bias_fix) + eps_adam),
    )


def local(
    tokens,
    cotangent,
    positions,
    owners,
    masters,
    basis_left,
    basis_right,
    moment1,
    moment2,
    ema,
    vectors,
    vector_moment1,
    vector_moment2,
    hidden_bias,
    hidden_moment1,
    hidden_moment2,
):
    length, width = tokens.shape
    slots = masters.shape[1]
    me = lax.axis_index("dp")
    column = lax.axis_index("mlp")
    replicas = lax.axis_size("dp") // 2
    place = jnp.stack([me, column, me // 2]).astype(jnp.int32)
    owner_row = owners[0]

    inverse_freq = 10000.0 ** (-(jnp.arange(ROT // 2, dtype=F32) * 2.0) / ROT)
    angles = inverse_freq[:, None] * positions.astype(F32)[None, :]
    table = jnp.concatenate([jnp.cos(angles), jnp.sin(angles)], axis=0)
    hats, cots, tables, attn_parts, own_attn, own_ff, send_ff = front(
        tokens, cotangent, table, masters[0], (owner_row // slots ^ me) * slots + owner_row % slots
    )

    mine, across, slab, reduced = middle(
        vectors,
        hidden_bias.reshape(2 * GROUP, -1),
        tables,
        hats,
        cots,
        own_attn,
        attn_parts,
        own_ff,
        send_ff,
        slots,
    )
    state = [item[0] for item in (basis_left, basis_right, moment1, moment2, masters, ema)]
    own_grad, first_new, second_new, master_new, weight_copy, ema_new = soap(
        place, owner_row, slab, state, replicas
    )
    result, grad_tokens = finish(tokens, cotangent, mine, across, vectors)
    vector_grad = jnp.concatenate([reduced[:8], reduced[7:8]], axis=0)
    hidden_grad = reduced[8:].reshape(FF)
    vec_first, vec_second, vectors_new = adam_step(
        vector_grad, vector_moment1, vector_moment2, vectors
    )
    hid_first, hid_second, hidden_new = adam_step(
        hidden_grad, hidden_moment1, hidden_moment2, hidden_bias
    )
    return (
        result,
        grad_tokens,
        own_grad[None],
        first_new[None],
        second_new[None],
        master_new[None],
        weight_copy[None],
        ema_new[None],
        vector_grad,
        vec_first,
        vec_second,
        vectors_new,
        hidden_grad,
        hid_first,
        hid_second,
        hidden_new,
    )


def solution(mesh):
    split = P(("dp", "mlp"), None)
    tiled = P("mlp", "dp", None, None)
    return jax.shard_map(
        local,
        mesh=mesh,
        in_specs=(split, split, P(("dp", "mlp")), P("mlp", None)) + (tiled,) * 6 + (P(),) * 6,
        out_specs=(split, split) + (tiled,) * 6 + (P(),) * 8,
        check_vma=False,
    )
```

time: 371 us -> 289 us (0.78)
  Pallas kernels: 329 us -> 276 us
  local copies, waits for them, and re-layouts: 32.8 us -> 1.38 us
    pallas_call x4 -> x2, Pallas kernels: 228 us -> 177 us  [the longest x1 170 us: middle(): pl.pallas_call(functools.partial(middle_kernel, slots, devices), out_shap...]
    unnamed x67 -> x15, local copies, waits for them, and re-layouts: 27.5 us -> 0.05 us
    pallas_call x1, Pallas kernels: 24.2 us -> 13.9 us  [soap(): pl.pallas_call(functools.partial(soap_kernel, slots, replicas, per_step),...]
    pallas_call x1, Pallas kernels: 76.4 us -> 85.7 us  [front(): pl.pallas_call(functools.partial(front_kernel, slots, devices), out_shape...]
where the time goes in v1:
time: 289 us; the launch traced here: 284 us
  Pallas kernels  276 us (96%)
  other arithmetic  4.66 us (2%)
    pallas_call x1, Pallas kernels, middle(): pl.pallas_call(functools.partial(middle_kernel, slots, devices), out_shap...  170 us
    pallas_call x1, Pallas kernels, front(): pl.pallas_call(functools.partial(front_kernel, slots, devices), out_shape...  85.7 us
    pallas_call x1, Pallas kernels, soap(): pl.pallas_call(functools.partial(soap_kernel, slots, replicas, per_step),...  13.9 us
    pallas_call x1, Pallas kernels, finish(): pl.pallas_call(finish_kernel, grid=(length // rows,), out_shape=[jax.Shap...  6.44 us

profile of v1, /device:TPU:7, one launch (start us, length us, event | category | flops | bytes accessed | tf_op | source)
XLA Modules:
  0.0 283.6 jit_solution(4201712493253106128)
XLA Ops:
  0.7 0.6 pad_add_fusion.refs_0_
  1.3 1.3 fusion.2.tile_ref
  2.5 0.7 convert_element_type.3
  3.2 1.3 reshape.46.refs_1_
  4.5 0.1 multiply_cosine_fusion
  4.7 0.6 pad_maximum_fusion.1.table
  5.3 85.7 %front.1 = (bf16[4,512,1024]{2,1,0:T(8,128)(2,1)}, bf16[4,512,1024]{2,1,0:T(8,128)(2,1)}, f32[4,16,512]{2,1,0:T(8,128)}, bf16[6144,128]{1,0:T(8,128)(2,1)}, bf16...) custom-call(f32[512,1024]{1,0:T(8,128)} %tokens.3, f32[512,1024]{1,0:T(8,128)} %cot.3, ...), custom_call_target="tpu_custom_call" | custom-call | bytes 209715200 | tf_op jit(solution)/shard_map/front/pallas_call | solution.py:298
  91.0 170.3 %middle.1 = (bf16[2,512,1024]{2,1,0:T(8,128)(2,1)}, bf16[2,512,1024]{2,1,0:T(8,128)(2,1)}, bf16[24576,128]{1,0:T(8,128)(2,1)}, f32[12,1024]{1,0:T(8,128)}) custom-call(f32[9,1024]{1,0:T(8,128)} %bias.1, f32[8,512]{1,0:T(8,128)} %reshape.46.refs_1_, f32[4,16,512]{2,1,0:T(8,128)} %get-tuple-element.35.refs_2_, ...), custom_call_target="tpu_custom_call" | custom-call | flops 60000002048 | bytes 41943040 | tf_op jit(solution)/shard_map/middle/pallas_call | solution.py:817
  261.3 0.0 copy-start.4
  261.3 0.0 copy-start.3
  261.3 0.0 copy-start.5
  261.3 0.0 copy-start.6
  261.4 0.0 copy-start
  261.4 0.0 copy-start.1
  261.4 0.0 copy-start.2
  261.4 6.4 %finish.1 = (f32[512,1024]{1,0:T(8,128)}, f32[512,1024]{1,0:T(8,128)}) custom-call(f32[512,1024]{1,0:T(8,128)} %tokens.3, f32[512,1024]{1,0:T(8,128)} %cot.3, bf16[2,512,1024]{2,1,0:T(8,128)(2,1)} %get-tuple-element.42.mine, bf16[2,512,1024]{2,1,0:T(8,128)(2,1)} %get-tuple-element.43.across, f32[9,1024]{1,0:T(8,128)} %bias.1), custom_call_target="tpu_custom_call" | custom-call | bytes 12582912 | tf_op jit(solution)/shard_map/finish/pallas_call | solution.py:1019
  267.8 0.0 copy-done.4
  267.9 0.0 copy-done.3
  267.9 0.0 copy-done.5
  267.9 0.0 copy-done.6
  267.9 0.6 divide_subtract_fusion.1
  268.5 0.0 copy-done
  268.5 0.0 copy-done.1
  268.5 0.0 copy-done.2
  268.5 0.7 divide_subtract_fusion
  269.3 13.9 %soap.1 = (f32[24,128,128]{2,1,0:T(8,128)}, f32[24,128,128]{2,1,0:T(8,128)}, f32[24,128,128]{2,1,0:T(8,128)}, f32[24,128,128]{2,1,0:T(8,128)}, bf16[24,128,128]{2,1,0:T(8,128)(2,1)}, /*index=5*/f32[24,128,128]{2,1,0:T(8,128)}) custom-call(s32[3]{0:T(128)} %pad_add_fusion.refs_0_, s32[192]{0:T(256)} %bitcast.29, ...), custom_call_target="tpu_custom_call" | custom-call | flops 2415919104 | bytes 20971520 | tf_op jit(solution)/shard_map/soap/pallas_call | solution.py:978
  (4 shorter events, 0.0 us)
Async XLA Ops:
  261.3 6.5 %copy-start.4 = (f32[12,1024]{1,0:T(8,128)S(1)}, f32[12,1024]{1,0:T(8,128)}, u32[]{:S(2)}) copy-start(f32[12,1024]{1,0:T(8,128)} %get-tuple-element.53) | copy-start | bytes 147460
  261.3 6.5 %copy-start.3 = (f32[4096]{0:T(1024)S(1)}, f32[4096]{0:T(1024)}, u32[]{:S(2)}) copy-start(f32[4096]{0:T(1024)} %param.29) | copy-start | bytes 49156
  261.3 6.5 %copy-start.5 = (f32[4096]{0:T(1024)S(1)}, f32[4096]{0:T(1024)}, u32[]{:S(2)}) copy-start(f32[4096]{0:T(1024)} %param.31) | copy-start | bytes 49156
  261.3 6.5 %copy-start.6 = (f32[4096]{0:T(1024)S(1)}, f32[4096]{0:T(1024)}, u32[]{:S(2)}) copy-start(f32[4096]{0:T(1024)} %param.30) | copy-start | bytes 49156
  261.4 7.2 %copy-start = (f32[9,1024]{1,0:T(8,128)S(1)}, f32[9,1024]{1,0:T(8,128)}, u32[]{:S(2)}) copy-start(f32[9,1024]{1,0:T(8,128)} %bias.1) | copy-start | bytes 110596
  261.4 7.2 %copy-start.1 = (f32[9,1024]{1,0:T(8,128)S(1)}, f32[9,1024]{1,0:T(8,128)}, u32[]{:S(2)}) copy-start(f32[9,1024]{1,0:T(8,128)} %param.28) | copy-start | bytes 110596
  261.4 7.2 %copy-start.2 = (f32[9,1024]{1,0:T(8,128)S(1)}, f32[9,1024]{1,0:T(8,128)}, u32[]{:S(2)}) copy-start(f32[9,1024]{1,0:T(8,128)} %param.27) | copy-start | bytes 110596
